TPU v7x, 256 devices: a whole 4x4x8 slice. The times are simulated.
256 devices in a mesh: seq: 32 (over y, x, core), ch: 8 (over z).
Axes of the slice: x: 4, y: 4, z: 8, core: 2. Of those that a mesh axis runs over, the one named last changes fastest.
Arguments:
- hidden_in: bfloat16 [8192, 32768], P('ch', 'seq'), may hold values from -6 to 6
- w_in: bfloat16 [8192, 384], P('ch'), may hold values from -0.0625 to 0.0625
- short_taps: float32 [3, 384], P(None, 'ch'), may hold values from -4 to 4
- rates: float32 [128, 16], P('ch'), may hold values from 1.5258789e-05 to 0.05
- residues: float32 [128, 16], P('ch'), may hold values from -3 to 3
- skip_gain: float32 [128], P('ch'), may hold values from -3 to 3
- w_out: bfloat16 [8192, 128], P('ch'), may hold values from -0.5 to 0.5
Outputs:
- mixed: bfloat16 [8192, 32768], P('ch', 'seq')
All inputs are finite; a program needn't handle non-finite values.
Results may differ from a plain program's by a relative error of at most 0.0075.
Values may be sent and summed in bfloat16 or wider, within the bound.
A program may use at most 64 MiB of HBM per device.

v0:
```python
import math

import jax
import jax.numpy as jnp
from jax import lax
from jax.sharding import PartitionSpec as P

precise = lax.Precision.HIGHEST


def partner_2(block, axis, bit):
    count = lax.axis_size(axis)
    route = []
    for low in range(count):
        high = low | 1 << bit
        if high != low and high < count:
            route += [(low, high), (high, low)]
    return lax.ppermute(block, axis, route)


def passed_along(value, axis, steps):
    count = lax.axis_size(axis)
    initial, last = (max(0, -steps), min(count, count - steps))
    return lax.ppermute(value, axis, [(source, source + steps) for source in range(initial, last)])


def phase_pair(left_index, right_index, period, direction):
    product = left_index * right_index % period
    phase_angle = 2.0 * math.pi / period * product.astype(jnp.float32)
    return (jnp.cos(phase_angle), direction * jnp.sin(phase_angle))


def complex_times(left_real, left_imag, right_real, right_imag):
    return (
        left_real * right_real - left_imag * right_imag,
        left_real * right_imag + left_imag * right_real,
    )


def square_pair(length, direction):
    row_index = lax.broadcasted_iota(jnp.int32, (length, length), 0)
    col_index = lax.broadcasted_iota(jnp.int32, (length, length), 1)
    return phase_pair(row_index, col_index, length, direction)


def along_last(real_part, imag_part, direction):
    leading = real_part.shape[:-1]
    length = real_part.shape[-1]
    outer_len = 1
    while outer_len * outer_len * 4 <= length and length % (2 * outer_len) == 0:
        outer_len = outer_len * 2
    inner_len = length // outer_len
    flat_real = real_part.reshape(-1, outer_len, inner_len)
    flat_imag = imag_part.reshape(-1, outer_len, inner_len)
    first_cos, first_sin = square_pair(outer_len, direction)
    section_real = jnp.einsum("ka,rab->rkb", first_cos, flat_real, precision=precise) - jnp.einsum(
        "ka,rab->rkb", first_sin, flat_imag, precision=precise
    )
    section_imag = jnp.einsum("ka,rab->rkb", first_sin, flat_real, precision=precise) + jnp.einsum(
        "ka,rab->rkb", first_cos, flat_imag, precision=precise
    )
    outer_index = lax.broadcasted_iota(jnp.int32, (outer_len, inner_len), 0)
    inner_index = lax.broadcasted_iota(jnp.int32, (outer_len, inner_len), 1)
    twist_cos, twist_sin = phase_pair(outer_index, inner_index, length, direction)
    section_real, section_imag = complex_times(section_real, section_imag, twist_cos, twist_sin)
    second_cos, second_sin = square_pair(inner_len, direction)
    final_real = jnp.einsum(
        "rkb,bm->rmk", section_real, second_cos, precision=precise
    ) - jnp.einsum("rkb,bm->rmk", section_imag, second_sin, precision=precise)
    final_imag = jnp.einsum(
        "rkb,bm->rmk", section_real, second_sin, precision=precise
    ) + jnp.einsum("rkb,bm->rmk", section_imag, second_cos, precision=precise)
    new_shape = leading + (length,)
    return (final_real.reshape(new_shape), final_imag.reshape(new_shape))


def bit_reverse(value, levels):
    result = jnp.zeros((), jnp.int32)
    for level_bit in range(levels):
        result = result + value // (1 << level_bit) % 2 * (1 << levels - 1 - level_bit)
    return result


def conv_butterfly(signal, kernel):
    seq_count = lax.axis_size("seq")
    my_rank = lax.axis_index("seq")
    channels, length = signal.shape
    levels = seq_count.bit_length() - 1
    total_len = 2 * seq_count * length
    stacked = jnp.stack([signal, kernel])
    shift_angle = math.pi / seq_count * my_rank.astype(jnp.float32)
    real_part = jnp.stack([stacked, stacked * jnp.cos(shift_angle)])
    imag_part = jnp.stack([jnp.zeros_like(stacked), -stacked * jnp.sin(shift_angle)])
    for level_bit in range(levels - 1, -1, -1):
        half_span = 1 << level_bit
        partner = partner_2(jnp.stack([real_part, imag_part]), "seq", level_bit)
        upper_side = my_rank // half_span % 2 == 1
        turn_angle = -(math.pi / half_span) * (my_rank % half_span).astype(jnp.float32)
        turn_real, turn_imag = complex_times(
            partner[0] - real_part, partner[1] - imag_part, jnp.cos(turn_angle), jnp.sin(turn_angle)
        )
        real_part = jnp.where(upper_side, turn_real, real_part + partner[0])
        imag_part = jnp.where(upper_side, turn_imag, imag_part + partner[1])
    reversed_rank = bit_reverse(my_rank, levels)
    k_outer = 2 * reversed_rank + lax.broadcasted_iota(jnp.int32, (2, 1, 1, length), 0)
    j_inner = lax.broadcasted_iota(jnp.int32, (2, 1, 1, length), 3)
    twist_cos, twist_sin = phase_pair(k_outer, j_inner, total_len, -1.0)
    real_part, imag_part = complex_times(real_part, imag_part, twist_cos, twist_sin)
    spec_real, spec_imag = along_last(real_part, imag_part, -1.0)
    prod_real, prod_imag = complex_times(
        spec_real[:, 0], spec_imag[:, 0], spec_real[:, 1], spec_imag[:, 1]
    )
    back_real, back_imag = along_last(prod_real, prod_imag, 1.0)
    undo_cos, undo_sin = phase_pair(k_outer[:, 0], j_inner[:, 0], total_len, 1.0)
    back_real, back_imag = complex_times(back_real, back_imag, undo_cos, undo_sin)
    for level_bit in range(levels):
        half_span = 1 << level_bit
        partner = partner_2(jnp.stack([back_real, back_imag]), "seq", level_bit)
        upper_side = my_rank // half_span % 2 == 1
        turn_angle = math.pi / half_span * (my_rank % half_span).astype(jnp.float32)
        turn_cos = jnp.cos(turn_angle)
        turn_sin = jnp.sin(turn_angle)
        from_partner = complex_times(partner[0], partner[1], turn_cos, turn_sin)
        from_mine = complex_times(back_real, back_imag, turn_cos, turn_sin)
        new_real = jnp.where(upper_side, partner[0] - from_mine[0], back_real + from_partner[0])
        new_imag = jnp.where(upper_side, partner[1] - from_mine[1], back_imag + from_partner[1])
        back_real, back_imag = (new_real, new_imag)
    combined = (
        back_real[0] + back_real[1] * jnp.cos(shift_angle) - back_imag[1] * jnp.sin(shift_angle)
    )
    return combined / total_len


def body(hidden_in, w_in, short_taps, rates, residues, skip_gain, w_out):
    my_rank = lax.axis_index("seq")
    width_local, length = hidden_in.shape
    row_count = w_in.shape[1] // lax.axis_size("ch")
    picked = w_in
    featurized = lax.psum_scatter(
        jnp.einsum("dm,dt->mt", picked, hidden_in, preferred_element_type=jnp.float32),
        "ch",
        scatter_dimension=0,
        tiled=True,
    ).astype(jnp.bfloat16)
    carried = passed_along(featurized[:, length - 2 :], "seq", 1)
    extended = jnp.concatenate([carried, featurized], axis=1).astype(jnp.float32)
    short = (
        short_taps[0][:, None] * extended[:, 2:]
        + short_taps[1][:, None] * extended[:, 1:-1]
        + short_taps[2][:, None] * extended[:, :-2]
    )
    grouped = short.reshape(row_count // 3, 3, length)
    query = grouped[:, 0]
    driven_low = lax.optimization_barrier((grouped[:, 1] * grouped[:, 2]).astype(jnp.bfloat16))
    driven = driven_low.astype(jnp.float32)
    positions = (my_rank * length + lax.broadcasted_iota(jnp.int32, (length,), 0)).astype(
        jnp.float32
    )
    decay = jnp.exp(-rates[:, :, None] * positions[None, None, :])
    impulse = jnp.sum((residues * jnp.sqrt(rates))[:, :, None] * decay, axis=1)
    long_conv = conv_butterfly(driven, impulse)
    gated = (query * (long_conv + skip_gain[:, None] * driven)).astype(jnp.bfloat16)
    picked = w_out
    mixed = jnp.dot(
        picked, lax.all_gather(gated, "ch", axis=0, tiled=True), preferred_element_type=jnp.float32
    )
    return mixed.astype(jnp.bfloat16)


def solution(mesh):
    in_specs = (
        P("ch", "seq"),
        P("ch", None),
        P(None, "ch"),
        P("ch", None),
        P("ch", None),
        P("ch"),
        P("ch", None),
    )
    out_specs = P("ch", "seq")
    return jax.shard_map(body, mesh=mesh, in_specs=in_specs, out_specs=out_specs, check_vma=False)
```

profile of v0, /device:TPU:24, one launch (start us, length us, event | category | flops | bytes accessed | tf_op | source)
XLA Modules:
  0.0 241.1 jit_solution(16963301798685388541)
XLA Ops:
  6.5 1.6 copy-done
  8.1 3.3 %fusion.204 = f32[384,1024]{1,0:T(8,128)} fusion(bf16[1024,384]{1,0:T(8,128)(2,1)} %param.8, bf16[1024,1024]{1,0:T(8,128)(2,1)S(1)} %copy-done), kind=kOutput, calls=%fused_computation.306 | convolution fusion | flops 805306368 | bytes 4456448 | tf_op jit(solution)/shard_map/dm,dt->mt/dot_general | solution.py:140
  12.1 42.5 %reduce-scatter.2.cloned.1.call-done = f32[48,1024]{1,0:T(8,128)} async-done(((f32[384,1024]{1,0:T(8,128)}), f32[48,1024]{1,0:T(8,128)}) %reduce-scatter.2.cloned.1.call-update) | async-done | bytes 196624 | tf_op jit(solution)/shard_map/reduce_scatter | solution.py:139
  55.6 1.9 collective-permute-start
  57.7 5.0 %collective-permute-done = bf16[48,2]{1,0:T(8,128)(2,1)S(1)} collective-permute-done((bf16[48,2]{1,0:T(8,128)(2,1)S(1)}, bf16[48,2]{1,0:T(8,128)(2,1)S(1)}, u32[]{:S(2)}, u32[]{:S(2)}) %collective-permute-start) | collective-permute-done | bytes 224 | tf_op jit(solution)/shard_map/ppermute | solution.py:24
  66.3 11.4 %collective-permute-done.1 = f32[2,2,2,16,1024]{4,3,2,1,0:T(8,128)S(1)} collective-permute-done((f32[2,2,2,16,1024]{4,3,2,1,0:T(8,128)S(1)}, f32[2,2,2,16,1024]{4,3,2,1,0:T(8,128)S(1)}, u32[]{:S(2)}, u32[]{:S(2)}) %collective-permute-start.1) | collective-permute-done | bytes 524320 | tf_op jit(solution)/shard_map/ppermute | solution.py:18
  79.4 8.4 %collective-permute-done.2 = f32[2,2,2,16,1024]{4,3,2,1,0:T(8,128)} collective-permute-done((f32[2,2,2,16,1024]{4,3,2,1,0:T(8,128)S(1)}, f32[2,2,2,16,1024]{4,3,2,1,0:T(8,128)}, u32[]{:S(2)}, u32[]{:S(2)}) %collective-permute-start.2) | collective-permute-done | bytes 524320 | tf_op jit(solution)/shard_map/ppermute | solution.py:18
  89.0 4.5 %collective-permute-start.3 = (f32[2,2,2,16,1024]{4,3,2,1,0:T(8,128)S(1)}, f32[2,2,2,16,1024]{4,3,2,1,0:T(8,128)}, u32[]{:S(2)}, u32[]{:S(2)}) collective-permute-start(f32[2,2,2,16,1024]{4,3,2,1,0:T(8,128)S(1)} %pad_maximum_fusion.2), channel_id=1, source_target_pairs={{0,32},{32,0},{8,40},{40,8},{16,48},{48,16},{24,56},{56,24},{64,96... | collective-permute-start | bytes 1572872 | tf_op jit(solution)/shard_map/ppermute | solution.py:18
  93.7 9.2 %collective-permute-done.3 = f32[2,2,2,16,1024]{4,3,2,1,0:T(8,128)} collective-permute-done((f32[2,2,2,16,1024]{4,3,2,1,0:T(8,128)S(1)}, f32[2,2,2,16,1024]{4,3,2,1,0:T(8,128)}, u32[]{:S(2)}, u32[]{:S(2)}) %collective-permute-start.3) | collective-permute-done | bytes 524320 | tf_op jit(solution)/shard_map/ppermute | solution.py:18
  104.8 2.6 %collective-permute-start.4 = (f32[2,2,2,16,1024]{4,3,2,1,0:T(8,128)}, f32[2,2,2,16,1024]{4,3,2,1,0:T(8,128)S(1)}, u32[]{:S(2)}, u32[]{:S(2)}) collective-permute-start(f32[2,2,2,16,1024]{4,3,2,1,0:T(8,128)} %pad_maximum_fusion.3), channel_id=1, source_target_pairs={{0,16},{16,0},{8,24},{24,8},{32,48},{48,32},{40,56},{56,40},{64,80... | collective-permute-start | bytes 1572872 | tf_op jit(solution)/shard_map/ppermute | solution.py:18
  107.6 8.6 %collective-permute-done.4 = f32[2,2,2,16,1024]{4,3,2,1,0:T(8,128)S(1)} collective-permute-done((f32[2,2,2,16,1024]{4,3,2,1,0:T(8,128)}, f32[2,2,2,16,1024]{4,3,2,1,0:T(8,128)S(1)}, u32[]{:S(2)}, u32[]{:S(2)}) %collective-permute-start.4) | collective-permute-done | bytes 524320 | tf_op jit(solution)/shard_map/ppermute | solution.py:18
  120.1 1.9 copy.54
  125.5 1.9 copy.56
  128.2 1.9 multiply_add_fusion.1
  131.9 1.7 fusion.5
  133.6 1.7 fusion.4
  135.3 2.0 copy.67
  137.7 2.0 copy.64
  142.1 2.0 fusion.73
  144.1 1.8 fusion.82
  146.9 2.0 fusion.2
  148.9 2.2 fusion.3
  156.0 2.5 %fusion.1 = f32[32,32,32]{2,1,0:T(8,128)} fusion(f32[32,32,32]{2,0,1:T(8,128)} %fusion.28, f32[32,32,32]{1,2,0:T(8,128)S(1)} %fusion.2, f32[32,32,32]{1,2,0:T(8,128)S(1)} %fusion.3, f32[32,32]{0,1:T(8,128)S(1)} %copy-done.9, f32[32,32]{0,1:T(8,128)S(1)} %get-tuple-element.57), kind=kOutput, calls=%fused_computation.4 | convolution fusion | flops 12728320 | bytes 532480 | tf_op jit(solution)/shard_map/rkb,bm->rmk/dot_general | solution.py:69
  163.0 1.7 collective-permute-start.7
  164.9 6.8 %collective-permute-done.7 = f32[2,2,16,1024]{3,2,1,0:T(8,128)} collective-permute-done((f32[2,2,16,1024]{3,2,1,0:T(8,128)}, f32[2,2,16,1024]{3,2,1,0:T(8,128)}, u32[]{:S(2)}, u32[]{:S(2)}) %collective-permute-start.7) | collective-permute-done | bytes 262176 | tf_op jit(solution)/shard_map/ppermute | solution.py:18
  174.1 2.0 collective-permute-start.8
  176.3 7.1 %collective-permute-done.8 = f32[2,2,16,1024]{3,2,1,0:T(8,128)S(1)} collective-permute-done((f32[2,2,16,1024]{3,2,1,0:T(8,128)}, f32[2,2,16,1024]{3,2,1,0:T(8,128)S(1)}, u32[]{:S(2)}, u32[]{:S(2)}) %collective-permute-start.8) | collective-permute-done | bytes 262176 | tf_op jit(solution)/shard_map/ppermute | solution.py:18
  188.2 4.6 %collective-permute-done.9 = f32[2,2,16,1024]{3,2,1,0:T(8,128)} collective-permute-done((f32[2,2,16,1024]{3,2,1,0:T(8,128)}, f32[2,2,16,1024]{3,2,1,0:T(8,128)}, u32[]{:S(2)}, u32[]{:S(2)}) %collective-permute-start.9) | collective-permute-done | bytes 262176 | tf_op jit(solution)/shard_map/ppermute | solution.py:18
  197.5 4.4 %collective-permute-done.10 = f32[2,2,16,1024]{3,2,1,0:T(8,128)S(1)} collective-permute-done((f32[2,2,16,1024]{3,2,1,0:T(8,128)S(1)}, f32[2,2,16,1024]{3,2,1,0:T(8,128)S(1)}, u32[]{:S(2)}, u32[]{:S(2)}) %collective-permute-start.10) | collective-permute-done | bytes 262176 | tf_op jit(solution)/shard_map/ppermute | solution.py:18
  203.3 24.9 %all_gather.3 = bf16[128,1024]{1,0:T(8,128)(2,1)S(1)} all-gather(bf16[16,1024]{1,0:T(8,128)(2,1)S(1)} %fusion.55), channel_id=1, replica_groups=mesh['seq'=32,'ch'=8] {'ch'}, dimensions={0}, use_global_device_ids=true | all-gather | bytes 294912 | tf_op jit(solution)/shard_map/all_gather | solution.py:165
  228.2 2.1 convert_bitcast_fusion
  230.3 3.9 %copy.80 = bf16[1024,1024]{1,0:T(8,128)(2,1)} copy(bf16[1024,1024]{0,1:T(8,128)(2,1)} %convert_bitcast_fusion) | data formatting | bytes 4194304 | tf_op jit(solution)/shard_map/convert_element_type | solution.py:167
  (115 shorter events, 45.3 us)
Async XLA Ops:
  6.5 1.6 copy-start
  6.5 4.9 %copy-start.17 = (f32[16,16]{1,0:T(8,128)S(1)}, f32[16,16]{1,0:T(8,128)}, u32[]{:S(2)}) copy-start(f32[16,16]{1,0:T(8,128)} %param.11) | copy-start | bytes 3076
  6.5 4.9 %copy-start.18 = (f32[16,16]{1,0:T(8,128)S(1)}, f32[16,16]{1,0:T(8,128)}, u32[]{:S(2)}) copy-start(f32[16,16]{1,0:T(8,128)} %param.10) | copy-start | bytes 3076
  6.5 48.1 %reduce-scatter.2.cloned.1.call-start = ((), (), s32[]{:S(2)}) async-start(), calls=%async_computation.1 | async-start | bytes 1769472 | tf_op jit(solution)/shard_map/reduce_scatter | solution.py:139
  11.4 0.7 copy-start.19
  55.6 7.1 %collective-permute-start = (bf16[48,2]{1,0:T(8,128)(2,1)S(1)}, bf16[48,2]{1,0:T(8,128)(2,1)S(1)}, u32[]{:S(2)}, u32[]{:S(2)}) collective-permute-start(bf16[48,2]{1,0:T(8,128)(2,1)S(1)} %slice.168), channel_id=1, source_target_pairs={{0,8},{8,16},{16,24},{24,32},{32,40},{40,48},{48,56},{56,64},{64,7... | collective-permute-start | bytes 584 | tf_op jit(solution)/shard_map/ppermute | solution.py:24
  64.5 13.1 %collective-permute-start.1 = (f32[2,2,2,16,1024]{4,3,2,1,0:T(8,128)S(1)}, f32[2,2,2,16,1024]{4,3,2,1,0:T(8,128)S(1)}, u32[]{:S(2)}, u32[]{:S(2)}) collective-permute-start(f32[2,2,2,16,1024]{4,3,2,1,0:T(8,128)S(1)} %pad_maximum_fusion), channel_id=1, source_target_pairs={{0,128},{128,0},{8,136},{136,8},{16,144},{144,16},{24,152},{152,24... | collective-permute-start | bytes 1572872 | tf_op jit(solution)/shard_map/ppermute | solution.py:18
  77.8 10.0 %collective-permute-start.2 = (f32[2,2,2,16,1024]{4,3,2,1,0:T(8,128)S(1)}, f32[2,2,2,16,1024]{4,3,2,1,0:T(8,128)}, u32[]{:S(2)}, u32[]{:S(2)}) collective-permute-start(f32[2,2,2,16,1024]{4,3,2,1,0:T(8,128)S(1)} %pad_maximum_fusion.1), channel_id=1, source_target_pairs={{0,64},{64,0},{8,72},{72,8},{16,80},{80,16},{24,88},{88,24},{32,96... | collective-permute-start | bytes 1572872 | tf_op jit(solution)/shard_map/ppermute | solution.py:18
  89.0 13.8 %collective-permute-start.3 = (f32[2,2,2,16,1024]{4,3,2,1,0:T(8,128)S(1)}, f32[2,2,2,16,1024]{4,3,2,1,0:T(8,128)}, u32[]{:S(2)}, u32[]{:S(2)}) collective-permute-start(f32[2,2,2,16,1024]{4,3,2,1,0:T(8,128)S(1)} %pad_maximum_fusion.2), channel_id=1, source_target_pairs={{0,32},{32,0},{8,40},{40,8},{16,48},{48,16},{24,56},{56,24},{64,96... | collective-permute-start | bytes 1572872 | tf_op jit(solution)/shard_map/ppermute | solution.py:18
  104.8 11.5 %collective-permute-start.4 = (f32[2,2,2,16,1024]{4,3,2,1,0:T(8,128)}, f32[2,2,2,16,1024]{4,3,2,1,0:T(8,128)S(1)}, u32[]{:S(2)}, u32[]{:S(2)}) collective-permute-start(f32[2,2,2,16,1024]{4,3,2,1,0:T(8,128)} %pad_maximum_fusion.3), channel_id=1, source_target_pairs={{0,16},{16,0},{8,24},{24,8},{32,48},{48,32},{40,56},{56,40},{64,80... | collective-permute-start | bytes 1572872 | tf_op jit(solution)/shard_map/ppermute | solution.py:18
  116.4 2.2 collective-permute-start.5
  118.3 3.7 %copy-start.14 = (f32[2,1024]{1,0:T(2,128)}, f32[2,1024]{1,0:T(2,128)S(1)}, u32[]{:S(2)}) copy-start(f32[2,1024]{1,0:T(2,128)S(1)} %get-tuple-element.53) | copy-start | bytes 24580
  145.9 5.2 %copy-start.9 = (f32[32,32]{0,1:T(8,128)S(1)}, f32[32,32]{0,1:T(8,128)}, u32[]{:S(2)}) copy-start(f32[32,32]{0,1:T(8,128)} %fusion.109) | copy-start | bytes 12292
  146.0 0.8 copy-start.1
  154.7 5.1 %copy-start.15 = (f32[2,1024]{1,0:T(2,128)S(1)}, f32[2,1024]{1,0:T(2,128)}, u32[]{:S(2)}) copy-start(f32[2,1024]{1,0:T(2,128)} %copy-done.14) | copy-start | bytes 24580
  154.7 5.1 %copy-start.16 = (f32[2,1024]{1,0:T(2,128)S(1)}, f32[2,1024]{1,0:T(2,128)}, u32[]{:S(2)}) copy-start(f32[2,1024]{1,0:T(2,128)} %get-tuple-element.51) | copy-start | bytes 24580
  159.9 27.2 %copy-start.2 = (f32[32,32,32]{2,1,0:T(8,128)S(1)}, f32[32,32,32]{2,1,0:T(8,128)}, u32[]{:S(2)}) copy-start(f32[32,32,32]{2,1,0:T(8,128)} %fusion) | copy-start | bytes 393220
  159.9 1.6 collective-permute-start.6
  161.5 0.7 copy-start.7
  162.3 25.7 %copy-start.3 = (f32[32,32,32]{2,1,0:T(8,128)S(1)}, f32[32,32,32]{2,1,0:T(8,128)}, u32[]{:S(2)}) copy-start(f32[32,32,32]{2,1,0:T(8,128)} %fusion.1) | copy-start | bytes 393220
  163.0 8.7 %collective-permute-start.7 = (f32[2,2,16,1024]{3,2,1,0:T(8,128)}, f32[2,2,16,1024]{3,2,1,0:T(8,128)}, u32[]{:S(2)}, u32[]{:S(2)}) collective-permute-start(f32[2,2,16,1024]{3,2,1,0:T(8,128)} %pad_maximum_fusion.7), channel_id=1, source_target_pairs={{0,16},{16,0},{8,24},{24,8},{32,48},{48,32},{40,56},{56,40},{64,80... | collective-permute-start | bytes 786440 | tf_op jit(solution)/shard_map/ppermute | solution.py:18
  172.8 0.7 copy-start.5
  172.8 1.4 copy-start.6
  174.1 9.3 %collective-permute-start.8 = (f32[2,2,16,1024]{3,2,1,0:T(8,128)}, f32[2,2,16,1024]{3,2,1,0:T(8,128)S(1)}, u32[]{:S(2)}, u32[]{:S(2)}) collective-permute-start(f32[2,2,16,1024]{3,2,1,0:T(8,128)} %pad_maximum_fusion.8), channel_id=1, source_target_pairs={{0,32},{32,0},{8,40},{40,8},{16,48},{48,16},{24,56},{56,24},{64,96... | collective-permute-start | bytes 786440 | tf_op jit(solution)/shard_map/ppermute | solution.py:18
  184.5 0.6 copy-start.4
  185.9 7.0 %collective-permute-start.9 = (f32[2,2,16,1024]{3,2,1,0:T(8,128)}, f32[2,2,16,1024]{3,2,1,0:T(8,128)}, u32[]{:S(2)}, u32[]{:S(2)}) collective-permute-start(f32[2,2,16,1024]{3,2,1,0:T(8,128)} %pad_maximum_fusion.9), channel_id=1, source_target_pairs={{0,64},{64,0},{8,72},{72,8},{16,80},{80,16},{24,88},{88,24},{32,96... | collective-permute-start | bytes 786440 | tf_op jit(solution)/shard_map/ppermute | solution.py:18
  188.0 7.4 %copy-start.8 = (f32[2,2,16,1024]{3,2,1,0:T(8,128)S(1)}, f32[2,2,16,1024]{3,2,1,0:T(8,128)}, u32[]{:S(2)}) copy-start(f32[2,2,16,1024]{3,2,1,0:T(8,128)} %copy-done.7) | copy-start | bytes 786436
  194.0 9.2 %copy-start.11 = (bf16[16,1,1024]{2,0,1:T(8,128)(2,1)S(1)}, bf16[16,1,1024]{2,0,1:T(8,128)(2,1)}, u32[]{:S(2)}) copy-start(bf16[16,1,1024]{2,0,1:T(8,128)(2,1)} %copy-done.10) | copy-start | bytes 98308
  194.0 9.2 %copy-start.13 = (f32[16,1,1024]{2,1,0:T(1,128)S(1)}, f32[16,1,1024]{2,1,0:T(1,128)}, u32[]{:S(2)}) copy-start(f32[16,1,1024]{2,1,0:T(1,128)} %get-tuple-element.40) | copy-start | bytes 196612
  194.0 9.2 %copy-start.20 = (f32[16]{0:T(128)S(1)}, f32[16]{0:T(128)}, u32[]{:S(2)}) copy-start(f32[16]{0:T(128)} %param.12) | copy-start | bytes 196
  194.0 8.0 %collective-permute-start.10 = (f32[2,2,16,1024]{3,2,1,0:T(8,128)S(1)}, f32[2,2,16,1024]{3,2,1,0:T(8,128)S(1)}, u32[]{:S(2)}, u32[]{:S(2)}) collective-permute-start(f32[2,2,16,1024]{3,2,1,0:T(8,128)S(1)} %pad_maximum_fusion.10), channel_id=1, source_target_pairs={{0,128},{128,0},{8,136},{136,8},{16,144},{144,16},{24,152},{152,24... | collective-permute-start | bytes 786440 | tf_op jit(solution)/shard_map/ppermute | solution.py:18
  196.4 31.8 %copy-start.12 = (bf16[1024,128]{1,0:T(8,128)(2,1)S(1)}, bf16[1024,128]{1,0:T(8,128)(2,1)}, u32[]{:S(2)}) copy-start(bf16[1024,128]{1,0:T(8,128)(2,1)} %param.13) | copy-start | bytes 786436
  (1 other events, 0.6 us)
Sparse Core Ops, SparseCore 0:
  11.5 43.0 reduce-scatter.1
where the time goes:
time: 243 us; the launch traced here: 241 us
  waiting for transfers between devices  110 us (45%)
  matrix products  29.4 us (12%)
  local copies, waits for them, and re-layouts  25.4 us (10%)
  blocking collectives  24.9 us (10%)
  starting transfers between devices  18.6 us (8%)
  other arithmetic  17.6 us (7%)
  between operations  15.5 us (6%)
    ppermute x10, waiting for transfers between devices, partner_2(): return lax.ppermute(block, axis, route)  62.2 us
    reduce_scatter x1, waiting for transfers between devices, body(): lax.psum_scatter(jnp.einsum('dm,dt->mt', picked, hidden_in, preferred_ele...  42.5 us
    all_gather x1, blocking collectives, body(): lax.all_gather(gated, 'ch', axis=0, tiled=True)  24.9 us
    ppermute x10, starting transfers between devices, partner_2(): return lax.ppermute(block, axis, route)  16.7 us
    select_n x6, other arithmetic, conv_butterfly(): jnp.where(upper_side, partner[0] - from_mine[0], back_real + from_partner...  5.42 us
    reshape x6, local copies, waits for them, and re-layouts, along_last(): return (final_real.reshape(new_shape), final_imag.reshape(new_shape))  5.39 us
    unnamed x43, local copies, waits for them, and re-layouts  5.1 us
    ppermute x1, waiting for transfers between devices, passed_along(): lax.ppermute(value, axis, [(source, source + steps) for source in range(i...  5.04 us
  transfers between devices with their start and end apart: 12, of which 12 were waited for; matrix products, arithmetic and copies ran while one was open for 2% of the time, Pallas kernels for 0%

commit v1 on v0

v1 whole, which is shorter than its diff:
```python
import functools

import jax
import jax.numpy as jnp
from jax import lax
from jax.experimental import pallas as pl
from jax.experimental.pallas import tpu as pltpu
from jax.sharding import PartitionSpec as P

MESH = pl.DeviceIdType.MESH
f32 = jnp.float32
bf16 = jnp.bfloat16
HIGH = lax.Precision.HIGHEST
NT = (((1,), (1,)), ((), ()))
NN = (((1,), (0,)), ((), ()))
CL = 128
ROW = 8


def mm(a, b, dims=NN, precision=None):
    return lax.dot_general(a, b, dims, precision=precision, preferred_element_type=f32)


def halves(x):
    hi = x.astype(bf16)
    return hi, (x - hi.astype(f32)).astype(bf16)


def iota(shape, dim):
    return lax.broadcasted_iota(jnp.int32, shape, dim)


def conv_kernel(
    n_seq,
    n_ch,
    hid,
    w_ref,
    taps_ref,
    rates_ref,
    res_ref,
    skip_ref,
    out_ref,
    hidv,
    wt,
    part,
    kv_s,
    kv_r,
    q_s,
    q_r,
    tot,
    halo_s,
    halo_r,
    gath,
    st0,
    st1,
    st2,
    par,
    e_hl,
    p_hl,
    tcat,
    dscr,
    yscr,
    xscr,
    load_sem,
    kv_ss,
    kv_rs,
    q_ss,
    q_rs,
    halo_ss,
    halo_rs,
    st1_ss,
    st1_rs,
    st2_ss,
    st2_rs,
    ag_ss,
    ag_rs,
):
    p = lax.axis_index("seq")
    z = lax.axis_index("ch")
    depth, length = hid.shape
    rows = w_ref.shape[1]
    per = rows // n_ch
    cs = per // 3
    nm = rates_ref.shape[1]
    st = cs * nm
    half = length // 2
    nk = length // CL
    quarter = length // 4
    row_y = p // ROW
    r = p % ROW
    n_y = n_seq // ROW

    def zz(k):
        return lax.rem(z + (k + n_ch), n_ch)

    ring = (zz(1), zz(-1))

    loads = []
    for i in (3, 2, 1, 0):
        cp = pltpu.make_async_copy(
            hid.at[:, pl.ds(i * quarter, quarter)],
            hidv.at[:, pl.ds(i * quarter, quarter)],
            load_sem.at[i],
        )
        cp.start()
        loads.append((i, cp))

    mates = [row_y * ROW + lax.rem(r + k, ROW) for k in range(1, ROW)]
    peers = [lax.rem(row_y + k, n_y) * ROW + r for k in range(1, n_y)]
    after = lax.rem(p + 1, n_seq)
    before = lax.rem(p + n_seq - 1, n_seq)
    barrier = pltpu.get_barrier_semaphore()
    for s in ring:
        pl.semaphore_signal(barrier, inc=1, device_id=(p, s), device_id_type=MESH)
    for s in mates + peers + [before]:
        pl.semaphore_signal(barrier, inc=1, device_id=(s, z), device_id_type=MESH)

    new = iota((rows, rows), 0)
    blk = (new * 1366) >> 16
    comp = (new - blk * per) >> 4
    old = blk * per + 3 * (new & (cs - 1)) + jnp.where(comp == 2, 0, comp + 1)
    perm = jnp.where(old == iota((rows, rows), 1), 1.0, 0.0).astype(bf16)
    wt[...] = mm(perm, w_ref[...], NT).astype(bf16)

    sends = []

    def remote(src, dst, ssem, rsem, dev):
        cp = pltpu.make_async_remote_copy(
            src_ref=src,
            dst_ref=dst,
            send_sem=ssem,
            recv_sem=rsem,
            device_id=dev,
            device_id_type=MESH,
        )
        cp.start()
        sends.append(cp)

    def arrived(dst, ssem, rsem):
        pltpu.make_async_remote_copy(
            src_ref=dst,
            dst_ref=dst,
            send_sem=ssem,
            recv_sem=rsem,
            device_id=(p, ring[0]),
            device_id_type=MESH,
        ).wait_recv()

    bufs = {
        "kv": (kv_s, kv_r, kv_ss, kv_rs, 0, 2 * cs),
        "q": (q_s, q_r, q_ss, q_rs, 2 * cs, cs),
    }
    toks = (pl.ds(0, half), pl.ds(half, half))

    def own(kind, h, d, dist):
        row0, n = bufs[kind][4:]
        dest = zz(dist if d == 0 else -dist)
        return part[dest, row0 : row0 + n, toks[h]]

    def send(kind, h, d, hop, value):
        sbuf, rbuf, ss, rs = bufs[kind][:4]
        sbuf[d, hop, h] = value.astype(bf16)
        remote(
            sbuf.at[d, hop, h], rbuf.at[d, hop, h], ss.at[d, hop, h], rs.at[d, hop, h], (p, ring[d])
        )

    def first(kind, h):
        long = 0 if h == 1 else 1
        send(kind, h, long, 0, own(kind, h, long, 4))
        send(kind, h, 1 - long, 1, own(kind, h, 1 - long, 3))

    def take(kind, h, d, hop):
        _, rbuf, ss, rs, row0, n = bufs[kind]
        arrived(rbuf.at[d, hop, h], ss.at[d, hop, h], rs.at[d, hop, h])
        got = rbuf[d, hop, h].astype(f32)
        if hop < 3:
            send(kind, h, d, hop + 1, got + own(kind, h, d, 3 - hop))
        elif (d == 0) == (h == 1):
            tot[row0 : row0 + n, toks[h]] = tot[row0 : row0 + n, toks[h]] + got
        else:
            tot[row0 : row0 + n, toks[h]] = part[z, row0 : row0 + n, toks[h]] + got

    def stage(kind, s, h):
        long = 0 if h == 1 else 1
        if s < 4:
            take(kind, h, 1 - long, s)
        take(kind, h, long, s - 1)

    for n, (i, cp) in enumerate(loads):
        cp.wait()
        tok = pl.ds(i * quarter, quarter)
        part[:, :, tok] = mm(wt[...], hidv[:, tok]).reshape(n_ch, per, quarter)
        if n == 1:
            pl.semaphore_wait(barrier, 3 + len(mates) + len(peers))
            first("kv", 1)
        if n == 3:
            first("kv", 0)

    lane_st = iota((cs, st), 1)
    mine = (lane_st >> 4) == iota((cs, st), 0)
    rep = jnp.where((iota((nm, st), 1) & (nm - 1)) == iota((nm, st), 0), 1.0, 0.0)

    def as_row(x):
        return jnp.sum(jnp.where(mine, mm(x, rep, precision=HIGH), 0.0), axis=0, keepdims=True)

    lam = as_row(rates_ref[...])
    gain = as_row(res_ref[...] * jnp.sqrt(rates_ref[...]))
    steps = iota((CL, st), 0).astype(f32)
    e_hi, e_lo = halves(jnp.exp(-lam * (CL - 1 - steps)))
    e_hl[0] = e_hi
    e_hl[1] = e_lo
    p_hi, p_lo = halves(gain * jnp.exp(-lam * (steps + 1.0)))
    p_hl[0] = p_hi
    p_hl[1] = p_lo

    stage("kv", 1, 1)
    stage("kv", 1, 0)
    first("q", 1)
    first("q", 0)

    spread = jnp.where(mine, gain, 0.0)
    taps0 = mm(spread, jnp.exp(-lam * steps), NT, HIGH)
    causal = iota((CL, CL), 1) >= iota((CL, CL), 0)

    def lay_out(c0, c1):
        for c in range(c0, c1):
            line = jnp.broadcast_to(taps0[c : c + 1, :], (CL, CL))
            tri = jnp.where(causal, pltpu.roll(line, 0, 1, stride=1, stride_axis=0), 0.0)
            hi, lo = halves(tri)
            tcat[c, 0:CL] = hi
            tcat[c, CL : 2 * CL] = lo

    lay_out(0, 8)
    lane_per = iota((cs, per), 1)
    row_per = iota((cs, per), 0)
    for i in range(3):
        line = jnp.broadcast_to(taps_ref[i : i + 1, :], (cs, per))
        for j in range(3):
            picked = jnp.where(lane_per == 3 * row_per + j, line, 0.0)
            par[3 * i + j] = jnp.broadcast_to(jnp.sum(picked, axis=1, keepdims=True), (cs, CL))
    skip_line = jnp.broadcast_to(skip_ref[...], (cs, cs))
    skip_col = jnp.sum(
        jnp.where(iota((cs, cs), 0) == iota((cs, cs), 1), skip_line, 0.0), axis=1, keepdims=True
    )

    stage("kv", 2, 1)
    stage("kv", 2, 0)
    stage("q", 1, 1)
    stage("q", 1, 0)
    lay_out(8, 16)
    decay_k = [jnp.exp(-lam * float(CL * k)) for k in range(nk)]
    rf = r.astype(f32)
    block = lam * float(length)
    w_own = jnp.exp(-block * (ROW - 1 - rf))
    w_before = [
        jnp.where(r >= k, jnp.exp(-block * float(k - 1)), 0.0) for k in range(1, ROW)
    ]
    w_row = [
        jnp.exp(-block * (ROW - 1 - lax.rem(r + ROW - k, ROW).astype(f32))) for k in range(1, ROW)
    ]
    w_rows = [
        jnp.where(row_y >= k, jnp.exp(-block * (rf + float(ROW * (k - 1)))), 0.0)
        for k in range(1, n_y)
    ]
    stage("kv", 3, 1)
    stage("kv", 3, 0)
    stage("q", 2, 1)
    stage("q", 2, 0)
    stage("kv", 4, 1)

    def tail(kind, i, row0, n):
        halo_s[row0 : row0 + n] = tot[row0 : row0 + n, length - CL : length].astype(bf16)
        remote(
            halo_s.at[pl.ds(row0, n)],
            halo_r.at[pl.ds(row0, n)],
            halo_ss.at[i],
            halo_rs.at[i],
            (after, z),
        )

    def tail_in(i, row0, n):
        arrived(halo_r.at[pl.ds(row0, n)], halo_ss.at[i], halo_rs.at[i])

    tail("kv", 0, 0, 2 * cs)
    stage("kv", 4, 0)

    def short(row0, j):
        edge = jnp.where(p > 0, halo_r[row0 : row0 + cs].astype(f32), 0.0)
        x = tot[row0 : row0 + cs]
        ext = jnp.concatenate([edge, x], axis=1)
        one = pltpu.roll(ext, 1, 1)[:, CL:]
        two = pltpu.roll(ext, 2, 1)[:, CL:]
        t = [par[3 * i + j][:, 0:1] for i in range(3)]
        return t[0] * x + t[1] * one + t[2] * two

    tail_in(0, 0, 2 * cs)
    driven = (short(0, 1) * short(cs, 2)).astype(bf16)
    stacked = jnp.concatenate([driven[:, CL * k : CL * (k + 1)] for k in range(nk)], axis=0)
    dscr[...] = stacked.astype(f32)
    states = mm(stacked, e_hl[0]) + mm(stacked, e_hl[1])
    carry = jnp.zeros((cs, st), f32)
    for k in range(nk):
        xscr[cs * k : cs * (k + 1)] = carry
        carry = decay_k[1] * carry + jnp.where(mine, states[cs * k : cs * (k + 1)], 0.0)
    total = jnp.sum(carry, axis=0, keepdims=True)
    st0[0] = total
    for k in range(1, ROW):
        remote(
            st0.at[0], st1.at[k - 1], st1_ss.at[k - 1], st1_rs.at[k - 1], (mates[k - 1], z)
        )

    stage("q", 3, 1)
    stage("q", 3, 0)
    for c in range(cs):
        line = dscr[pl.ds(c, nk, stride=cs), :].astype(bf16)
        yscr[pl.ds(c, nk, stride=cs), :] = mm(jnp.concatenate([line, line], axis=1), tcat[c])

    into = jnp.zeros((1, st), f32)
    whole = w_own * total
    for k in range(1, ROW):
        arrived(st1.at[k - 1], st1_ss.at[k - 1], st1_rs.at[k - 1])
        got = st1[k - 1]
        into = into + w_before[k - 1] * got
        whole = whole + w_row[k - 1] * got
    st0[1] = whole
    for k in range(1, n_y):
        remote(
            st0.at[1], st2.at[k - 1], st2_ss.at[k - 1], st2_rs.at[k - 1], (peers[k - 1], z)
        )
    stage("q", 4, 1)
    tail("q", 1, 2 * cs, cs)
    stage("q", 4, 0)
    tail_in(1, 2 * cs, cs)
    query = short(2 * cs, 0)
    for k in range(1, n_y):
        arrived(st2.at[k - 1], st2_ss.at[k - 1], st2_rs.at[k - 1])
        into = into + w_rows[k - 1] * st2[k - 1]
    wide = jnp.where(mine, into, 0.0)
    x = jnp.concatenate(
        [xscr[cs * k : cs * (k + 1)] + decay_k[k] * wide for k in range(nk)], axis=0
    )
    x_hi, x_lo = halves(x)
    y = yscr[...] + mm(x_hi, p_hl[0], NT) + mm(x_lo, p_hl[0], NT) + mm(x_hi, p_hl[1], NT)
    for k in range(nk):
        sl = slice(cs * k, cs * (k + 1))
        tok = slice(CL * k, CL * (k + 1))
        value = query[:, tok] * (y[sl] + skip_col * dscr[sl])
        gath[z, :, tok] = value.astype(bf16)

    def pass_on(src, h, d, hop):
        ref = gath.at[src, :, toks[h]]
        remote(ref, ref, ag_ss.at[d, hop, h], ag_rs.at[d, hop, h], (p, ring[d]))

    for h in (0, 1):
        for d in (0, 1):
            pass_on(z, h, d, 0)
    out_ref[z] = gath[z]
    for hop in range(4):
        for h in (0, 1):
            for d in (0, 1):
                if hop == 3 and (d == 0) != (h == 1):
                    continue
                src = zz(-hop - 1 if d == 0 else hop + 1)
                arrived(gath.at[src, :, toks[h]], ag_ss.at[d, hop, h], ag_rs.at[d, hop, h])
                if hop < 2 or (hop == 2 and (d == 0) == (h == 1)):
                    pass_on(src, h, d, hop + 1)
                out_ref[src, :, toks[h]] = gath[src, :, toks[h]]
    for cp in sends:
        cp.wait_send()


def solution(mesh):
    n_seq, n_ch = mesh.shape["seq"], mesh.shape["ch"]

    def body(hidden_in, w_in, short_taps, rates, residues, skip_gain, w_out):
        depth, length = hidden_in.shape
        rows = w_in.shape[1]
        per = rows // n_ch
        cs = per // 3
        st = cs * rates.shape[1]
        half = length // 2
        nk = length // CL
        n_y = n_seq // ROW
        vmem = pl.BlockSpec(memory_space=pltpu.VMEM)
        dma = pltpu.SemaphoreType.DMA
        gathered = pl.pallas_call(
            functools.partial(conv_kernel, n_seq, n_ch),
            out_shape=jax.ShapeDtypeStruct((n_ch, cs, length), bf16),
            in_specs=[pl.BlockSpec(memory_space=pl.ANY)] + [vmem] * 5,
            out_specs=vmem,
            scratch_shapes=[
                pltpu.VMEM((depth, length), bf16),
                pltpu.VMEM((rows, depth), bf16),
                pltpu.VMEM((n_ch, per, length), f32),
                pltpu.VMEM((2, 4, 2, 2 * cs, half), bf16),
                pltpu.VMEM((2, 4, 2, 2 * cs, half), bf16),
                pltpu.VMEM((2, 4, 2, cs, half), bf16),
                pltpu.VMEM((2, 4, 2, cs, half), bf16),
                pltpu.VMEM((per, length), f32),
                pltpu.VMEM((per, CL), bf16),
                pltpu.VMEM((per, CL), bf16),
                pltpu.VMEM((n_ch, cs, length), bf16),
                pltpu.VMEM((2, 1, st), f32),
                pltpu.VMEM((ROW - 1, 1, st), f32),
                pltpu.VMEM((n_y - 1, 1, st), f32),
                pltpu.VMEM((9, cs, CL), f32),
                pltpu.VMEM((2, CL, st), bf16),
                pltpu.VMEM((2, CL, st), bf16),
                pltpu.VMEM((cs, 2 * CL, CL), bf16),
                pltpu.VMEM((nk * cs, CL), f32),
                pltpu.VMEM((nk * cs, CL), f32),
                pltpu.VMEM((nk * cs, st), f32),
                dma((4,)),
                dma((2, 4, 2)),
                dma((2, 4, 2)),
                dma((2, 4, 2)),
                dma((2, 4, 2)),
                dma((2,)),
                dma((2,)),
                dma((ROW - 1,)),
                dma((ROW - 1,)),
                dma((n_y - 1,)),
                dma((n_y - 1,)),
                dma((2, 4, 2)),
                dma((2, 4, 2)),
            ],
            compiler_params=pltpu.CompilerParams(
                collective_id=0, has_side_effects=True, vmem_limit_bytes=40 * 1024 * 1024
            ),
        )(hidden_in, w_in, short_taps, rates, residues, skip_gain.reshape(1, cs))
        mixed = jnp.dot(w_out, gathered.reshape(n_ch * cs, length), preferred_element_type=f32)
        return mixed.astype(bf16)

    in_specs = (
        P("ch", "seq"),
        P("ch", None),
        P(None, "ch"),
        P("ch", None),
        P("ch", None),
        P("ch"),
        P("ch", None),
    )
    return jax.shard_map(
        body, mesh=mesh, in_specs=in_specs, out_specs=P("ch", "seq"), check_vma=False
    )
```

time: 243 us -> 53.1 us (0.22)
  waiting for transfers between devices: 110 us -> 0 us
  Pallas kernels: 0 us -> 43.4 us
  matrix products: 29.4 us -> 0.74 us
  blocking collectives: 24.9 us -> 0 us
  starting transfers between devices: 18.6 us -> 0 us
  other arithmetic: 17.6 us -> 0 us
  local copies, waits for them, and re-layouts: 25.4 us -> 8.06 us
  between operations: 15.5 us -> 0.03 us
    ppermute x11 -> x0, waiting for transfers between devices: 67.2 us -> none  [the longest x10 62.2 us: partner_2(): return lax.ppermute(block, axis, route)]
    pallas_call x0 -> x1, Pallas kernels: none -> 43.4 us  [body(): pl.pallas_call(functools.partial(conv_kernel, n_seq, n_ch), out_shape=jax...]
    reduce_scatter x1 -> x0, waiting for transfers between devices: 42.5 us -> none  [body(): lax.psum_scatter(jnp.einsum('dm,dt->mt', picked, hidden_in, preferred_ele...]
    dot_general x18 -> x1, matrix products: 29.4 us -> 0.74 us  [body(): jnp.dot(w_out, gathered.reshape(n_ch * cs, length), preferred_element_typ...]
    all_gather x1 -> x0, blocking collectives: 24.9 us -> none  [body(): lax.all_gather(gated, 'ch', axis=0, tiled=True)]
    ppermute x11 -> x0, starting transfers between devices: 18.6 us -> none  [the longest x10 16.7 us: partner_2(): return lax.ppermute(block, axis, route)]
    reshape x11 -> x0, local copies, waits for them, and re-layouts: 12 us -> none  [the longest x6 5.39 us: along_last(): return (final_real.reshape(new_shape), final_imag.reshape(new_shape))]
    select_n x11 -> x0, other arithmetic: 9.06 us -> none  [the longest x6 5.42 us: conv_butterfly(): jnp.where(upper_side, partner[0] - from_mine[0], back_real + from_partner...]
  transfers between devices with their start and end apart: 12 -> 0, of which waited for: 12 -> 0; matrix products, arithmetic and copies ran while one was open for 2% -> 0% of each run, Pallas kernels for 0% -> 0%
where the time goes in v1:
time: 53.1 us; the launch traced here: 52.3 us
  Pallas kernels  43.4 us (82%)
  local copies, waits for them, and re-layouts  8.06 us (15%)
  matrix products  0.74 us (1%)
    pallas_call x1, Pallas kernels, body(): pl.pallas_call(functools.partial(conv_kernel, n_seq, n_ch), out_shape=jax...  43.4 us
    unnamed x14, local copies, waits for them, and re-layouts  5.5 us
    convert_element_type x1, local copies, waits for them, and re-layouts, body(): return mixed.astype(bf16)  2.56 us

profile of v1, /device:TPU:24, one launch (start us, length us, event | category | flops | bytes accessed | tf_op | source)
XLA Modules:
  0.0 52.3 jit_solution(1721818337010588401)
XLA Ops:
  0.0 0.0 copy-start
  0.0 0.0 copy-start.1
  0.0 1.6 %copy-done.1 = bf16[1024,1024]{1,0:T(8,128)(2,1)S(1)} copy-done((bf16[1024,1024]{1,0:T(8,128)(2,1)S(1)}, bf16[1024,1024]{1,0:T(8,128)(2,1)}, u32[]{:S(2)}) %copy-start.1) | copy-done | bytes 2097176
  1.6 0.0 copy-start.2
  1.6 1.1 %copy-done.2 = bf16[1024,384]{1,0:T(8,128)(2,1)S(1)} copy-done((bf16[1024,384]{1,0:T(8,128)(2,1)S(1)}, bf16[1024,384]{1,0:T(8,128)(2,1)}, u32[]{:S(2)}) %copy-start.2) | copy-done | bytes 786456
  2.8 0.0 copy-start.3
  2.8 0.7 %copy-done.3 = f32[16,16]{1,0:T(8,128)S(1)} copy-done((f32[16,16]{1,0:T(8,128)S(1)}, f32[16,16]{1,0:T(8,128)}, u32[]{:S(2)}) %copy-start.3) | copy-done | bytes 1048
  3.5 0.0 copy-start.4
  3.5 0.7 %copy-done.4 = f32[16,16]{1,0:T(8,128)S(1)} copy-done((f32[16,16]{1,0:T(8,128)S(1)}, f32[16,16]{1,0:T(8,128)}, u32[]{:S(2)}) %copy-start.4) | copy-done | bytes 1048
  4.2 0.0 copy-start.5
  4.2 0.7 %copy-done.5 = f32[3,48]{1,0:T(4,128)S(1)} copy-done((f32[3,48]{1,0:T(4,128)S(1)}, f32[3,48]{1,0:T(4,128)}, u32[]{:S(2)}) %copy-start.5) | copy-done | bytes 600
  4.8 0.0 copy-start.6
  4.9 0.7 %copy-done.6 = f32[16]{0:T(128)S(1)} copy-done((f32[16]{0:T(128)S(1)}, f32[16]{0:T(128)}, u32[]{:S(2)}) %copy-start.6) | copy-done | bytes 88
  5.5 43.4 %shard_map.73 = bf16[8,16,1024]{2,1,0:T(8,128)(2,1)S(1)} custom-call(bf16[1024,1024]{1,0:T(8,128)(2,1)S(1)} %copy-done.1, bf16[1024,384]{1,0:T(8,128)(2,1)S(1)} %copy-done.2, f32[3,48]{1,0:T(4,128)S(1)} %copy-done.5, f32[16,16]{1,0:T(8,128)S(1)} %copy-done.3, f32[16,16]{1,0:T(8,128)S(1)} %copy-done.4, f32[1,16]{1,0:T(1,128)S(1)} %bitcast.7), custom_call_target="tpu_custom_call" | custom-call | tf_op jit(solution)/shard_map/pallas_call | solution.py:386
  49.0 0.0 copy-done
  49.0 0.7 %convert_bitcast_fusion = bf16[1024,1024]{0,1:T(8,128)(2,1)S(1)} fusion(bf16[128,1024]{1,0:T(8,128)(2,1)S(1)} %bitcast.6, bf16[1024,128]{1,0:T(8,128)(2,1)S(1)} %copy-done), kind=kOutput, calls=%fused_computation | convolution fusion | flops 269484032 | bytes 2621440 | tf_op jit(solution)/shard_map/dot_general | solution.py:431
  49.7 2.6 %copy.8 = bf16[1024,1024]{1,0:T(8,128)(2,1)} copy(bf16[1024,1024]{0,1:T(8,128)(2,1)S(1)} %convert_bitcast_fusion) | data formatting | bytes 4194304 | tf_op jit(solution)/shard_map/convert_element_type | solution.py:432
Async XLA Ops:
  0.0 49.0 %copy-start = (bf16[1024,128]{1,0:T(8,128)(2,1)S(1)}, bf16[1024,128]{1,0:T(8,128)(2,1)}, u32[]{:S(2)}) copy-start(bf16[1024,128]{1,0:T(8,128)(2,1)} %param.13) | copy-start | bytes 786436
  0.0 1.6 %copy-start.1 = (bf16[1024,1024]{1,0:T(8,128)(2,1)S(1)}, bf16[1024,1024]{1,0:T(8,128)(2,1)}, u32[]{:S(2)}) copy-start(bf16[1024,1024]{1,0:T(8,128)(2,1)} %hid.1) | copy-start | bytes 6291460
  1.6 1.1 %copy-start.2 = (bf16[1024,384]{1,0:T(8,128)(2,1)S(1)}, bf16[1024,384]{1,0:T(8,128)(2,1)}, u32[]{:S(2)}) copy-start(bf16[1024,384]{1,0:T(8,128)(2,1)} %w_ref.1) | copy-start | bytes 2359300
  2.8 0.7 %copy-start.3 = (f32[16,16]{1,0:T(8,128)S(1)}, f32[16,16]{1,0:T(8,128)}, u32[]{:S(2)}) copy-start(f32[16,16]{1,0:T(8,128)} %rates_ref.1) | copy-start | bytes 3076
  3.5 0.7 %copy-start.4 = (f32[16,16]{1,0:T(8,128)S(1)}, f32[16,16]{1,0:T(8,128)}, u32[]{:S(2)}) copy-start(f32[16,16]{1,0:T(8,128)} %res_ref.1) | copy-start | bytes 3076
  4.2 0.7 %copy-start.5 = (f32[3,48]{1,0:T(4,128)S(1)}, f32[3,48]{1,0:T(4,128)}, u32[]{:S(2)}) copy-start(f32[3,48]{1,0:T(4,128)} %taps_ref.1) | copy-start | bytes 1732
  4.8 0.7 %copy-start.6 = (f32[16]{0:T(128)S(1)}, f32[16]{0:T(128)}, u32[]{:S(2)}) copy-start(f32[16]{0:T(128)} %param.12) | copy-start | bytes 196

commit v2 on v1

--- a/solution.py
+++ b/solution.py
@@ -34,12 +34,17 @@
     n_seq,
     n_ch,
     hid,
+    w_in,
+    taps_in,
+    rates_in,
+    res_in,
+    skip_in,
+    out_ref,
     w_ref,
     taps_ref,
     rates_ref,
     res_ref,
     skip_ref,
-    out_ref,
     hidv,
     wt,
     part,
@@ -62,6 +67,7 @@
     yscr,
     xscr,
     load_sem,
+    small_sem,
     kv_ss,
     kv_rs,
     q_ss,
@@ -94,7 +100,15 @@
         return lax.rem(z + (k + n_ch), n_ch)
 
     ring = (zz(1), zz(-1))
-
+    sends = []
+    pending = {}
+
+    smalls = []
+    pairs = ((w_in, w_ref), (rates_in, rates_ref), (res_in, res_ref), (taps_in, taps_ref), (skip_in, skip_ref))
+    for i, (src, dst) in enumerate(pairs):
+        cp = pltpu.make_async_copy(src, dst, small_sem.at[i])
+        smalls.append(cp)
+    smalls[0].start()
     loads = []
     for i in (3, 2, 1, 0):
         cp = pltpu.make_async_copy(
@@ -104,13 +118,15 @@
         )
         cp.start()
         loads.append((i, cp))
+    for cp in smalls[1:]:
+        cp.start()
 
     mates = [row_y * ROW + lax.rem(r + k, ROW) for k in range(1, ROW)]
     peers = [lax.rem(row_y + k, n_y) * ROW + r for k in range(1, n_y)]
     after = lax.rem(p + 1, n_seq)
     before = lax.rem(p + n_seq - 1, n_seq)
     barrier = pltpu.get_barrier_semaphore()
-    for s in ring:
+    for s in ring + (zz(2), zz(-2)):
         pl.semaphore_signal(barrier, inc=1, device_id=(p, s), device_id_type=MESH)
     for s in mates + peers + [before]:
         pl.semaphore_signal(barrier, inc=1, device_id=(s, z), device_id_type=MESH)
@@ -120,11 +136,10 @@
     comp = (new - blk * per) >> 4
     old = blk * per + 3 * (new & (cs - 1)) + jnp.where(comp == 2, 0, comp + 1)
     perm = jnp.where(old == iota((rows, rows), 1), 1.0, 0.0).astype(bf16)
+    smalls[0].wait()
     wt[...] = mm(perm, w_ref[...], NT).astype(bf16)
 
-    sends = []
-
-    def remote(src, dst, ssem, rsem, dev):
+    def remote(key, src, dst, ssem, rsem, dev):
         cp = pltpu.make_async_remote_copy(
             src_ref=src,
             dst_ref=dst,
@@ -135,8 +150,10 @@
         )
         cp.start()
         sends.append(cp)
-
-    def arrived(dst, ssem, rsem):
+        pending[key] = (dst, ssem, rsem)
+
+    def arrived(key, dst, ssem, rsem):
+        pending.pop(key)
         pltpu.make_async_remote_copy(
             src_ref=dst,
             dst_ref=dst,
@@ -161,7 +178,12 @@
         sbuf, rbuf, ss, rs = bufs[kind][:4]
         sbuf[d, hop, h] = value.astype(bf16)
         remote(
-            sbuf.at[d, hop, h], rbuf.at[d, hop, h], ss.at[d, hop, h], rs.at[d, hop, h], (p, ring[d])
+            (kind, d, hop, h),
+            sbuf.at[d, hop, h],
+            rbuf.at[d, hop, h],
+            ss.at[d, hop, h],
+            rs.at[d, hop, h],
+            (p, ring[d]),
         )
 
     def first(kind, h):
@@ -171,7 +193,7 @@
 
     def take(kind, h, d, hop):
         _, rbuf, ss, rs, row0, n = bufs[kind]
-        arrived(rbuf.at[d, hop, h], ss.at[d, hop, h], rs.at[d, hop, h])
+        arrived((kind, d, hop, h), rbuf.at[d, hop, h], ss.at[d, hop, h], rs.at[d, hop, h])
         got = rbuf[d, hop, h].astype(f32)
         if hop < 3:
             send(kind, h, d, hop + 1, got + own(kind, h, d, 3 - hop))
@@ -191,7 +213,7 @@
         tok = pl.ds(i * quarter, quarter)
         part[:, :, tok] = mm(wt[...], hidv[:, tok]).reshape(n_ch, per, quarter)
         if n == 1:
-            pl.semaphore_wait(barrier, 3 + len(mates) + len(peers))
+            pl.semaphore_wait(barrier, 5 + len(mates) + len(peers))
             first("kv", 1)
         if n == 3:
             first("kv", 0)
@@ -203,6 +225,8 @@
     def as_row(x):
         return jnp.sum(jnp.where(mine, mm(x, rep, precision=HIGH), 0.0), axis=0, keepdims=True)
 
+    for cp in smalls[1:]:
+        cp.wait()
     lam = as_row(rates_ref[...])
     gain = as_row(res_ref[...] * jnp.sqrt(rates_ref[...]))
     steps = iota((CL, st), 0).astype(f32)
@@ -271,6 +295,7 @@
     def tail(kind, i, row0, n):
         halo_s[row0 : row0 + n] = tot[row0 : row0 + n, length - CL : length].astype(bf16)
         remote(
+            ("halo", i),
             halo_s.at[pl.ds(row0, n)],
             halo_r.at[pl.ds(row0, n)],
             halo_ss.at[i],
@@ -279,7 +304,7 @@
         )
 
     def tail_in(i, row0, n):
-        arrived(halo_r.at[pl.ds(row0, n)], halo_ss.at[i], halo_rs.at[i])
+        arrived(("halo", i), halo_r.at[pl.ds(row0, n)], halo_ss.at[i], halo_rs.at[i])
 
     tail("kv", 0, 0, 2 * cs)
     stage("kv", 4, 0)
@@ -306,7 +331,12 @@
     st0[0] = total
     for k in range(1, ROW):
         remote(
-            st0.at[0], st1.at[k - 1], st1_ss.at[k - 1], st1_rs.at[k - 1], (mates[k - 1], z)
+            ("st1", k),
+            st0.at[0],
+            st1.at[k - 1],
+            st1_ss.at[k - 1],
+            st1_rs.at[k - 1],
+            (mates[k - 1], z),
         )
 
     stage("q", 3, 1)
@@ -318,14 +348,19 @@
     into = jnp.zeros((1, st), f32)
     whole = w_own * total
     for k in range(1, ROW):
-        arrived(st1.at[k - 1], st1_ss.at[k - 1], st1_rs.at[k - 1])
+        arrived(("st1", k), st1.at[k - 1], st1_ss.at[k - 1], st1_rs.at[k - 1])
         got = st1[k - 1]
         into = into + w_before[k - 1] * got
         whole = whole + w_row[k - 1] * got
     st0[1] = whole
     for k in range(1, n_y):
         remote(
-            st0.at[1], st2.at[k - 1], st2_ss.at[k - 1], st2_rs.at[k - 1], (peers[k - 1], z)
+            ("st2", k),
+            st0.at[1],
+            st2.at[k - 1],
+            st2_ss.at[k - 1],
+            st2_rs.at[k - 1],
+            (peers[k - 1], z),
         )
     stage("q", 4, 1)
     tail("q", 1, 2 * cs, cs)
@@ -333,7 +368,7 @@
     tail_in(1, 2 * cs, cs)
     query = short(2 * cs, 0)
     for k in range(1, n_y):
-        arrived(st2.at[k - 1], st2_ss.at[k - 1], st2_rs.at[k - 1])
+        arrived(("st2", k), st2.at[k - 1], st2_ss.at[k - 1], st2_rs.at[k - 1])
         into = into + w_rows[k - 1] * st2[k - 1]
     wide = jnp.where(mine, into, 0.0)
     x = jnp.concatenate(
@@ -347,26 +382,50 @@
         value = query[:, tok] * (y[sl] + skip_col * dscr[sl])
         gath[z, :, tok] = value.astype(bf16)
 
-    def pass_on(src, h, d, hop):
-        ref = gath.at[src, :, toks[h]]
-        remote(ref, ref, ag_ss.at[d, hop, h], ag_rs.at[d, hop, h], (p, ring[d]))
-
-    for h in (0, 1):
+    hand_on = ((0, 2, None), (0, 1, None), (2, 1, None), (2, 2, 0))
+
+    def piece(i, d, dist):
+        part_of = hand_on[i][2]
+        tok = slice(None) if part_of is None else toks[part_of if d == 0 else 1 - part_of]
+        return gath.at[zz(-dist if d == 0 else dist), :, tok]
+
+    def hand(i, d):
+        hold, step, _ = hand_on[i]
+        ref = piece(i, d, hold)
+        target = (p, zz(step if d == 0 else -step))
+        remote(("ag", d, i), ref, ref, ag_ss.at[d, i], ag_rs.at[d, i], target)
+
+    def handed(i, d):
+        hold, step, _ = hand_on[i]
+        arrived(("ag", d, i), piece(i, d, hold + step), ag_ss.at[d, i], ag_rs.at[d, i])
+
+    for i in (0, 1):
         for d in (0, 1):
-            pass_on(z, h, d, 0)
-    out_ref[z] = gath[z]
-    for hop in range(4):
-        for h in (0, 1):
-            for d in (0, 1):
-                if hop == 3 and (d == 0) != (h == 1):
-                    continue
-                src = zz(-hop - 1 if d == 0 else hop + 1)
-                arrived(gath.at[src, :, toks[h]], ag_ss.at[d, hop, h], ag_rs.at[d, hop, h])
-                if hop < 2 or (hop == 2 and (d == 0) == (h == 1)):
-                    pass_on(src, h, d, hop + 1)
-                out_ref[src, :, toks[h]] = gath[src, :, toks[h]]
+            hand(i, d)
+    for d in (0, 1):
+        handed(0, d)
+        hand(2, d)
+        hand(3, d)
+    for i in (1, 2, 3):
+        for d in (0, 1):
+            handed(i, d)
+    out_ref[...] = gath[...]
     for cp in sends:
         cp.wait_send()
+
+
+def project_kernel(w_ref, x_ref, out, rows_ref, sem):
+    count = sem.shape[0]
+    tile = out.shape[0] // count
+    copies = []
+    for i in range(count):
+        at = pl.ds(i * tile, tile)
+        rows_ref[at] = mm(w_ref[at], x_ref[...]).astype(bf16)
+        cp = pltpu.make_async_copy(rows_ref.at[at], out.at[at], sem.at[i])
+        cp.start()
+        copies.append(cp)
+    for cp in copies:
+        cp.wait()
 
 
 def solution(mesh):
@@ -386,9 +445,14 @@
         gathered = pl.pallas_call(
             functools.partial(conv_kernel, n_seq, n_ch),
             out_shape=jax.ShapeDtypeStruct((n_ch, cs, length), bf16),
-            in_specs=[pl.BlockSpec(memory_space=pl.ANY)] + [vmem] * 5,
+            in_specs=[pl.BlockSpec(memory_space=pltpu.HBM)] * 6,
             out_specs=vmem,
             scratch_shapes=[
+                pltpu.VMEM(w_in.shape, bf16),
+                pltpu.VMEM(short_taps.shape, f32),
+                pltpu.VMEM(rates.shape, f32),
+                pltpu.VMEM(residues.shape, f32),
+                pltpu.VMEM((1, cs), f32),
                 pltpu.VMEM((depth, length), bf16),
                 pltpu.VMEM((rows, depth), bf16),
                 pltpu.VMEM((n_ch, per, length), f32),
@@ -411,6 +475,7 @@
                 pltpu.VMEM((nk * cs, CL), f32),
                 pltpu.VMEM((nk * cs, st), f32),
                 dma((4,)),
+                dma((5,)),
                 dma((2, 4, 2)),
                 dma((2, 4, 2)),
                 dma((2, 4, 2)),
@@ -421,15 +486,27 @@
                 dma((ROW - 1,)),
                 dma((n_y - 1,)),
                 dma((n_y - 1,)),
-                dma((2, 4, 2)),
-                dma((2, 4, 2)),
+                dma((2, 4)),
+                dma((2, 4)),
             ],
             compiler_params=pltpu.CompilerParams(
                 collective_id=0, has_side_effects=True, vmem_limit_bytes=40 * 1024 * 1024
             ),
-        )(hidden_in, w_in, short_taps, rates, residues, skip_gain.reshape(1, cs))
-        mixed = jnp.dot(w_out, gathered.reshape(n_ch * cs, length), preferred_element_type=f32)
-        return mixed.astype(bf16)
+        )(
+            *(
+                pltpu.with_memory_space_constraint(x, pltpu.HBM)
+                for x in (hidden_in, w_in, short_taps, rates, residues, skip_gain.reshape(1, cs))
+            )
+        )
+        slab = n_ch * cs
+        return pl.pallas_call(
+            project_kernel,
+            out_shape=jax.ShapeDtypeStruct((w_out.shape[0], length), bf16),
+            in_specs=[vmem] * 2,
+            out_specs=pl.BlockSpec(memory_space=pl.ANY),
+            scratch_shapes=[pltpu.VMEM((w_out.shape[0], length), bf16), dma((8,))],
+            compiler_params=pltpu.CompilerParams(vmem_limit_bytes=16 * 1024 * 1024),
+        )(w_out, gathered.reshape(slab, length))
 
     in_specs = (
         P("ch", "seq"),

time: 53.1 us -> 41.9 us (0.79)
  the two profiles are of different devices: /device:TPU:24 before, /device:TPU:32 now
where the time goes in v2:
time: 41.9 us; the launch traced here: 41.8 us
  Pallas kernels  41.8 us (100%)
    pallas_call x1, Pallas kernels, body(): pl.pallas_call(functools.partial(conv_kernel, n_seq, n_ch), out_shape=jax...  40.2 us
    pallas_call x1, Pallas kernels, body(): pl.pallas_call(project_kernel, out_shape=jax.ShapeDtypeStruct((w_out.shap...  1.59 us

profile of v2, /device:TPU:32, one launch (start us, length us, event | category | flops | bytes accessed | tf_op | source)
XLA Modules:
  0.0 41.8 jit_solution(13268695314672238317)
XLA Ops:
  0.0 0.0 copy-start
  0.0 40.2 %shard_map.73 = bf16[8,16,1024]{2,1,0:T(8,128)(2,1)S(1)} custom-call(bf16[1024,1024]{1,0:T(8,128)(2,1)} %hid.1, bf16[1024,384]{1,0:T(8,128)(2,1)} %w_in.1, f32[3,48]{1,0:T(4,128)} %taps_in.1, f32[16,16]{1,0:T(8,128)} %rates_in.1, f32[16,16]{1,0:T(8,128)} %res_in.1, f32[1,16]{1,0:T(1,128)} %bitcast.3), custom_call_target="tpu_custom_call" | custom-call | tf_op jit(solution)/shard_map/pallas_call | solution.py:445
  40.2 0.0 copy-done
  40.2 1.6 %shard_map.74 = bf16[1024,1024]{1,0:T(8,128)(2,1)} custom-call(bf16[1024,128]{1,0:T(8,128)(2,1)S(1)} %copy-done, bf16[128,1024]{1,0:T(8,128)(2,1)S(1)} %bitcast.2), custom_call_target="tpu_custom_call" | custom-call | tf_op jit(solution)/shard_map/pallas_call | solution.py:502
Async XLA Ops:
  0.0 40.2 %copy-start = (bf16[1024,128]{1,0:T(8,128)(2,1)S(1)}, bf16[1024,128]{1,0:T(8,128)(2,1)}, u32[]{:S(2)}) copy-start(bf16[1024,128]{1,0:T(8,128)(2,1)} %w_ref.1) | copy-start | bytes 786436

commit v3 on v2

--- a/solution.py
+++ b/solution.py
@@ -14,7 +14,6 @@
 NT = (((1,), (1,)), ((), ()))
 NN = (((1,), (0,)), ((), ()))
 CL = 128
-ROW = 8
 
 
 def mm(a, b, dims=NN, precision=None):
@@ -58,7 +57,6 @@
     gath,
     st0,
     st1,
-    st2,
     par,
     e_hl,
     p_hl,
@@ -74,10 +72,8 @@
     q_rs,
     halo_ss,
     halo_rs,
-    st1_ss,
-    st1_rs,
-    st2_ss,
-    st2_rs,
+    st_ss,
+    st_rs,
     ag_ss,
     ag_rs,
 ):
@@ -92,14 +88,14 @@
     half = length // 2
     nk = length // CL
     quarter = length // 4
-    row_y = p // ROW
-    r = p % ROW
-    n_y = n_seq // ROW
+    py, px, pc = p // 8, p // 2 % 4, p % 2
+    n_y = n_seq // 8
 
     def zz(k):
         return lax.rem(z + (k + n_ch), n_ch)
 
     ring = (zz(1), zz(-1))
+    ring2 = (zz(2), zz(-2))
     sends = []
     pending = {}
 
@@ -121,14 +117,16 @@
     for cp in smalls[1:]:
         cp.start()
 
-    mates = [row_y * ROW + lax.rem(r + k, ROW) for k in range(1, ROW)]
-    peers = [lax.rem(row_y + k, n_y) * ROW + r for k in range(1, n_y)]
+    def place(dy, dx, dc):
+        return lax.rem(py + dy + n_y, n_y) * 8 + lax.rem(px + dx + 4, 4) * 2 + lax.rem(pc + dc, 2)
+
+    moves = [(dy, dx, dc) for dy in range(n_y) for dx in range(4) for dc in range(2)][1:]
+    moves.sort(key=lambda m: (-min(m[0], n_y - m[0]) - min(m[1], 4 - m[1]), -m[2]))
     after = lax.rem(p + 1, n_seq)
-    before = lax.rem(p + n_seq - 1, n_seq)
     barrier = pltpu.get_barrier_semaphore()
-    for s in ring + (zz(2), zz(-2)):
+    for s in ring + ring2:
         pl.semaphore_signal(barrier, inc=1, device_id=(p, s), device_id_type=MESH)
-    for s in mates + peers + [before]:
+    for s in [place(*move) for move in moves]:
         pl.semaphore_signal(barrier, inc=1, device_id=(s, z), device_id_type=MESH)
 
     new = iota((rows, rows), 0)
@@ -174,49 +172,59 @@
         dest = zz(dist if d == 0 else -dist)
         return part[dest, row0 : row0 + n, toks[h]]
 
-    def send(kind, h, d, hop, value):
+    def send(kind, h, d, m, value):
         sbuf, rbuf, ss, rs = bufs[kind][:4]
-        sbuf[d, hop, h] = value.astype(bf16)
+        sbuf[d, m, h] = value.astype(bf16)
         remote(
-            (kind, d, hop, h),
-            sbuf.at[d, hop, h],
-            rbuf.at[d, hop, h],
-            ss.at[d, hop, h],
-            rs.at[d, hop, h],
-            (p, ring[d]),
-        )
-
-    def first(kind, h):
+            (kind, d, m, h),
+            sbuf.at[d, m, h],
+            rbuf.at[d, m, h],
+            ss.at[d, m, h],
+            rs.at[d, m, h],
+            (p, (ring, ring2)[m in (0, 2)][d]),
+        )
+
+    def far(kind, h):
+        send(kind, h, 0 if h == 1 else 1, 0, own(kind, h, 0 if h == 1 else 1, 4))
+        for d in (0, 1):
+            send(kind, h, d, 1, own(kind, h, d, 3))
+
+    def near(kind, h):
+        for d in (0, 1):
+            send(kind, h, d, 3, own(kind, h, d, 1))
+
+    def take(kind, h, d, m):
+        _, rbuf, ss, rs = bufs[kind][:4]
+        arrived((kind, d, m, h), rbuf.at[d, m, h], ss.at[d, m, h], rs.at[d, m, h])
+        return rbuf[d, m, h].astype(f32)
+
+    def merge(kind, h):
         long = 0 if h == 1 else 1
-        send(kind, h, long, 0, own(kind, h, long, 4))
-        send(kind, h, 1 - long, 1, own(kind, h, 1 - long, 3))
-
-    def take(kind, h, d, hop):
-        _, rbuf, ss, rs, row0, n = bufs[kind]
-        arrived((kind, d, hop, h), rbuf.at[d, hop, h], ss.at[d, hop, h], rs.at[d, hop, h])
-        got = rbuf[d, hop, h].astype(f32)
-        if hop < 3:
-            send(kind, h, d, hop + 1, got + own(kind, h, d, 3 - hop))
-        elif (d == 0) == (h == 1):
-            tot[row0 : row0 + n, toks[h]] = tot[row0 : row0 + n, toks[h]] + got
-        else:
-            tot[row0 : row0 + n, toks[h]] = part[z, row0 : row0 + n, toks[h]] + got
-
-    def stage(kind, s, h):
-        long = 0 if h == 1 else 1
-        if s < 4:
-            take(kind, h, 1 - long, s)
-        take(kind, h, long, s - 1)
+        for d in (1 - long, long):
+            value = own(kind, h, d, 2) + take(kind, h, d, 1)
+            if d == long:
+                value = value + take(kind, h, d, 0)
+            send(kind, h, d, 2, value)
+
+    def total_of(kind, h):
+        row0, n = bufs[kind][4:]
+        value = part[z, row0 : row0 + n, toks[h]]
+        for m in (3, 2):
+            for d in (0, 1):
+                value = value + take(kind, h, d, m)
+        tot[row0 : row0 + n, toks[h]] = value
 
     for n, (i, cp) in enumerate(loads):
         cp.wait()
         tok = pl.ds(i * quarter, quarter)
         part[:, :, tok] = mm(wt[...], hidv[:, tok]).reshape(n_ch, per, quarter)
         if n == 1:
-            pl.semaphore_wait(barrier, 5 + len(mates) + len(peers))
-            first("kv", 1)
+            pl.semaphore_wait(barrier, 4 + len(moves))
+            far("kv", 1)
         if n == 3:
-            first("kv", 0)
+            far("kv", 0)
+            far("q", 1)
+            far("q", 0)
 
     lane_st = iota((cs, st), 1)
     mine = (lane_st >> 4) == iota((cs, st), 0)
@@ -237,10 +245,9 @@
     p_hl[0] = p_hi
     p_hl[1] = p_lo
 
-    stage("kv", 1, 1)
-    stage("kv", 1, 0)
-    first("q", 1)
-    first("q", 0)
+    for h in (1, 0):
+        merge("kv", h)
+        near("kv", h)
 
     spread = jnp.where(mine, gain, 0.0)
     taps0 = mm(spread, jnp.exp(-lam * steps), NT, HIGH)
@@ -267,30 +274,19 @@
         jnp.where(iota((cs, cs), 0) == iota((cs, cs), 1), skip_line, 0.0), axis=1, keepdims=True
     )
 
-    stage("kv", 2, 1)
-    stage("kv", 2, 0)
-    stage("q", 1, 1)
-    stage("q", 1, 0)
+    for h in (1, 0):
+        merge("q", h)
+        near("q", h)
     lay_out(8, 16)
     decay_k = [jnp.exp(-lam * float(CL * k)) for k in range(nk)]
-    rf = r.astype(f32)
     block = lam * float(length)
-    w_own = jnp.exp(-block * (ROW - 1 - rf))
-    w_before = [
-        jnp.where(r >= k, jnp.exp(-block * float(k - 1)), 0.0) for k in range(1, ROW)
-    ]
-    w_row = [
-        jnp.exp(-block * (ROW - 1 - lax.rem(r + ROW - k, ROW).astype(f32))) for k in range(1, ROW)
-    ]
-    w_rows = [
-        jnp.where(row_y >= k, jnp.exp(-block * (rf + float(ROW * (k - 1)))), 0.0)
-        for k in range(1, n_y)
-    ]
-    stage("kv", 3, 1)
-    stage("kv", 3, 0)
-    stage("q", 2, 1)
-    stage("q", 2, 0)
-    stage("kv", 4, 1)
+    weight = []
+    for dy, dx, dc in moves:
+        src = place(-dy, -dx, dc)
+        weight.append(
+            jnp.where(src < p, jnp.exp(-block * jnp.maximum(p - 1 - src, 0).astype(f32)), 0.0)
+        )
+    total_of("kv", 1)
 
     def tail(kind, i, row0, n):
         halo_s[row0 : row0 + n] = tot[row0 : row0 + n, length - CL : length].astype(bf16)
@@ -307,7 +303,7 @@
         arrived(("halo", i), halo_r.at[pl.ds(row0, n)], halo_ss.at[i], halo_rs.at[i])
 
     tail("kv", 0, 0, 2 * cs)
-    stage("kv", 4, 0)
+    total_of("kv", 0)
 
     def short(row0, j):
         edge = jnp.where(p > 0, halo_r[row0 : row0 + cs].astype(f32), 0.0)
@@ -328,48 +324,25 @@
         xscr[cs * k : cs * (k + 1)] = carry
         carry = decay_k[1] * carry + jnp.where(mine, states[cs * k : cs * (k + 1)], 0.0)
     total = jnp.sum(carry, axis=0, keepdims=True)
-    st0[0] = total
-    for k in range(1, ROW):
+    st0[...] = total
+    for i, move in enumerate(moves):
         remote(
-            ("st1", k),
-            st0.at[0],
-            st1.at[k - 1],
-            st1_ss.at[k - 1],
-            st1_rs.at[k - 1],
-            (mates[k - 1], z),
-        )
-
-    stage("q", 3, 1)
-    stage("q", 3, 0)
+            ("st", i), st0, st1.at[i], st_ss.at[i], st_rs.at[i], (place(*move), z)
+        )
+
     for c in range(cs):
         line = dscr[pl.ds(c, nk, stride=cs), :].astype(bf16)
         yscr[pl.ds(c, nk, stride=cs), :] = mm(jnp.concatenate([line, line], axis=1), tcat[c])
 
-    into = jnp.zeros((1, st), f32)
-    whole = w_own * total
-    for k in range(1, ROW):
-        arrived(("st1", k), st1.at[k - 1], st1_ss.at[k - 1], st1_rs.at[k - 1])
-        got = st1[k - 1]
-        into = into + w_before[k - 1] * got
-        whole = whole + w_row[k - 1] * got
-    st0[1] = whole
-    for k in range(1, n_y):
-        remote(
-            ("st2", k),
-            st0.at[1],
-            st2.at[k - 1],
-            st2_ss.at[k - 1],
-            st2_rs.at[k - 1],
-            (peers[k - 1], z),
-        )
-    stage("q", 4, 1)
+    total_of("q", 1)
     tail("q", 1, 2 * cs, cs)
-    stage("q", 4, 0)
+    total_of("q", 0)
     tail_in(1, 2 * cs, cs)
     query = short(2 * cs, 0)
-    for k in range(1, n_y):
-        arrived(("st2", k), st2.at[k - 1], st2_ss.at[k - 1], st2_rs.at[k - 1])
-        into = into + w_rows[k - 1] * st2[k - 1]
+    into = jnp.zeros((1, st), f32)
+    for i in reversed(range(len(moves))):
+        arrived(("st", i), st1.at[i], st_ss.at[i], st_rs.at[i])
+        into = into + weight[i] * st1[i]
     wide = jnp.where(mine, into, 0.0)
     x = jnp.concatenate(
         [xscr[cs * k : cs * (k + 1)] + decay_k[k] * wide for k in range(nk)], axis=0
@@ -439,7 +412,6 @@
         st = cs * rates.shape[1]
         half = length // 2
         nk = length // CL
-        n_y = n_seq // ROW
         vmem = pl.BlockSpec(memory_space=pltpu.VMEM)
         dma = pltpu.SemaphoreType.DMA
         gathered = pl.pallas_call(
@@ -464,9 +436,8 @@
                 pltpu.VMEM((per, CL), bf16),
                 pltpu.VMEM((per, CL), bf16),
                 pltpu.VMEM((n_ch, cs, length), bf16),
-                pltpu.VMEM((2, 1, st), f32),
-                pltpu.VMEM((ROW - 1, 1, st), f32),
-                pltpu.VMEM((n_y - 1, 1, st), f32),
+                pltpu.VMEM((1, st), f32),
+                pltpu.VMEM((n_seq - 1, 1, st), f32),
                 pltpu.VMEM((9, cs, CL), f32),
                 pltpu.VMEM((2, CL, st), bf16),
                 pltpu.VMEM((2, CL, st), bf16),
@@ -482,10 +453,8 @@
                 dma((2, 4, 2)),
                 dma((2,)),
                 dma((2,)),
-                dma((ROW - 1,)),
-                dma((ROW - 1,)),
-                dma((n_y - 1,)),
-                dma((n_y - 1,)),
+                dma((n_seq - 1,)),
+                dma((n_seq - 1,)),
                 dma((2, 4)),
                 dma((2, 4)),
             ],

time: 41.9 us -> 37 us (0.88)
  Pallas kernels: 41.8 us -> 36.9 us
    pallas_call x1, Pallas kernels: 40.2 us -> 35.3 us  [body(): pl.pallas_call(functools.partial(conv_kernel, n_seq, n_ch), out_shape=jax...]
where the time goes in v3:
time: 37 us; the launch traced here: 36.9 us
  Pallas kernels  36.9 us (100%)
    pallas_call x1, Pallas kernels, body(): pl.pallas_call(functools.partial(conv_kernel, n_seq, n_ch), out_shape=jax...  35.3 us
    pallas_call x1, Pallas kernels, body(): pl.pallas_call(project_kernel, out_shape=jax.ShapeDtypeStruct((w_out.shap...  1.59 us

profile of v3, /device:TPU:32, one launch (start us, length us, event | category | flops | bytes accessed | tf_op | source)
XLA Modules:
  0.0 36.9 jit_solution(15607465936417836791)
XLA Ops:
  0.0 0.0 copy-start
  0.0 35.3 %shard_map.73 = bf16[8,16,1024]{2,1,0:T(8,128)(2,1)S(1)} custom-call(bf16[1024,1024]{1,0:T(8,128)(2,1)} %hid.1, bf16[1024,384]{1,0:T(8,128)(2,1)} %w_in.1, f32[3,48]{1,0:T(4,128)} %taps_in.1, f32[16,16]{1,0:T(8,128)} %rates_in.1, f32[16,16]{1,0:T(8,128)} %res_in.1, f32[1,16]{1,0:T(1,128)} %bitcast.3), custom_call_target="tpu_custom_call" | custom-call | tf_op jit(solution)/shard_map/pallas_call | solution.py:417
  35.3 0.0 copy-done
  35.3 1.6 %shard_map.74 = bf16[1024,1024]{1,0:T(8,128)(2,1)} custom-call(bf16[1024,128]{1,0:T(8,128)(2,1)S(1)} %copy-done, bf16[128,1024]{1,0:T(8,128)(2,1)S(1)} %bitcast.2), custom_call_target="tpu_custom_call" | custom-call | tf_op jit(solution)/shard_map/pallas_call | solution.py:471
Async XLA Ops:
  0.0 35.3 %copy-start = (bf16[1024,128]{1,0:T(8,128)(2,1)S(1)}, bf16[1024,128]{1,0:T(8,128)(2,1)}, u32[]{:S(2)}) copy-start(bf16[1024,128]{1,0:T(8,128)(2,1)} %w_ref.1) | copy-start | bytes 786436

commit v4 on v3

--- a/solution.py
+++ b/solution.py
@@ -66,15 +66,11 @@
     xscr,
     load_sem,
     small_sem,
-    kv_ss,
+    sent,
     kv_rs,
-    q_ss,
     q_rs,
-    halo_ss,
     halo_rs,
-    st_ss,
     st_rs,
-    ag_ss,
     ag_rs,
 ):
     p = lax.axis_index("seq")
@@ -88,15 +84,12 @@
     half = length // 2
     nk = length // CL
     quarter = length // 4
-    py, px, pc = p // 8, p // 2 % 4, p % 2
-    n_y = n_seq // 8
 
     def zz(k):
         return lax.rem(z + (k + n_ch), n_ch)
 
     ring = (zz(1), zz(-1))
     ring2 = (zz(2), zz(-2))
-    sends = []
     pending = {}
 
     smalls = []
@@ -117,17 +110,16 @@
     for cp in smalls[1:]:
         cp.start()
 
-    def place(dy, dx, dc):
-        return lax.rem(py + dy + n_y, n_y) * 8 + lax.rem(px + dx + 4, 4) * 2 + lax.rem(pc + dc, 2)
-
-    moves = [(dy, dx, dc) for dy in range(n_y) for dx in range(4) for dc in range(2)][1:]
-    moves.sort(key=lambda m: (-min(m[0], n_y - m[0]) - min(m[1], 4 - m[1]), -m[2]))
+    def hops(k):
+        return (0, 1, 2, 1)[k >> 1 & 3] + (0, 1, 2, 1)[k >> 3]
+
+    moves = sorted(range(1, n_seq), key=lambda k: -hops(k))
     after = lax.rem(p + 1, n_seq)
     barrier = pltpu.get_barrier_semaphore()
     for s in ring + ring2:
         pl.semaphore_signal(barrier, inc=1, device_id=(p, s), device_id_type=MESH)
-    for s in [place(*move) for move in moves]:
-        pl.semaphore_signal(barrier, inc=1, device_id=(s, z), device_id_type=MESH)
+    for k in moves:
+        pl.semaphore_signal(barrier, inc=1, device_id=(p ^ k, z), device_id_type=MESH)
 
     new = iota((rows, rows), 0)
     blk = (new * 1366) >> 16
@@ -138,32 +130,34 @@
     wt[...] = mm(perm, w_ref[...], NT).astype(bf16)
 
     def remote(key, src, dst, ssem, rsem, dev):
-        cp = pltpu.make_async_remote_copy(
+        pltpu.make_async_remote_copy(
             src_ref=src,
             dst_ref=dst,
             send_sem=ssem,
             recv_sem=rsem,
             device_id=dev,
             device_id_type=MESH,
-        )
-        cp.start()
-        sends.append(cp)
-        pending[key] = (dst, ssem, rsem)
-
-    def arrived(key, dst, ssem, rsem):
-        pending.pop(key)
-        pltpu.make_async_remote_copy(
-            src_ref=dst,
-            dst_ref=dst,
-            send_sem=ssem,
-            recv_sem=rsem,
+        ).start()
+        pending[key] = (dst, rsem)
+
+    def waiter(ref, sem):
+        return pltpu.make_async_remote_copy(
+            src_ref=ref,
+            dst_ref=ref,
+            send_sem=sem,
+            recv_sem=sem,
             device_id=(p, ring[0]),
             device_id_type=MESH,
-        ).wait_recv()
+        )
+
+    def arrived(keys, ref, sem):
+        for key in keys:
+            pending.pop(key)
+        waiter(ref, sem).wait_recv()
 
     bufs = {
-        "kv": (kv_s, kv_r, kv_ss, kv_rs, 0, 2 * cs),
-        "q": (q_s, q_r, q_ss, q_rs, 2 * cs, cs),
+        "kv": (kv_s, kv_r, sent.at[0], kv_rs, 0, 2 * cs),
+        "q": (q_s, q_r, sent.at[1], q_rs, 2 * cs, cs),
     }
     toks = (pl.ds(0, half), pl.ds(half, half))
 
@@ -172,20 +166,25 @@
         dest = zz(dist if d == 0 else -dist)
         return part[dest, row0 : row0 + n, toks[h]]
 
+    def long_way(h):
+        return 0 if h == 1 else 1
+
     def send(kind, h, d, m, value):
         sbuf, rbuf, ss, rs = bufs[kind][:4]
-        sbuf[d, m, h] = value.astype(bf16)
-        remote(
-            (kind, d, m, h),
-            sbuf.at[d, m, h],
-            rbuf.at[d, m, h],
-            ss.at[d, m, h],
-            rs.at[d, m, h],
-            (p, (ring, ring2)[m in (0, 2)][d]),
-        )
+        slot = (0, 1, 3, 5)[m] if d == long_way(h) else (None, 2, 4, 6)[m]
+        sbuf[h, slot] = value.astype(bf16)
+        to = (ring2, ring)[m % 2][d]
+        got = rs.at[h, (0, 0, 1, 2, 2, 2, 2)[slot]]
+        remote((kind, h, slot), sbuf.at[h, slot], rbuf.at[h, slot], ss, got, (p, to))
+
+    def take(kind, h, group, first, count):
+        _, rbuf, _, rs = bufs[kind][:4]
+        keys = [(kind, h, first + i) for i in range(count)]
+        arrived(keys, rbuf.at[h, pl.ds(first, count)], rs.at[h, group])
+        return [rbuf[h, first + i].astype(f32) for i in range(count)]
 
     def far(kind, h):
-        send(kind, h, 0 if h == 1 else 1, 0, own(kind, h, 0 if h == 1 else 1, 4))
+        send(kind, h, long_way(h), 0, own(kind, h, long_way(h), 4))
         for d in (0, 1):
             send(kind, h, d, 1, own(kind, h, d, 3))
 
@@ -193,25 +192,21 @@
         for d in (0, 1):
             send(kind, h, d, 3, own(kind, h, d, 1))
 
-    def take(kind, h, d, m):
-        _, rbuf, ss, rs = bufs[kind][:4]
-        arrived((kind, d, m, h), rbuf.at[d, m, h], ss.at[d, m, h], rs.at[d, m, h])
-        return rbuf[d, m, h].astype(f32)
-
-    def merge(kind, h):
-        long = 0 if h == 1 else 1
-        for d in (1 - long, long):
-            value = own(kind, h, d, 2) + take(kind, h, d, 1)
-            if d == long:
-                value = value + take(kind, h, d, 0)
-            send(kind, h, d, 2, value)
+    def merge_short(kind, h):
+        d = 1 - long_way(h)
+        (got,) = take(kind, h, 1, 2, 1)
+        send(kind, h, d, 2, own(kind, h, d, 2) + got)
+
+    def merge_long(kind, h):
+        d = long_way(h)
+        four, three = take(kind, h, 0, 0, 2)
+        send(kind, h, d, 2, own(kind, h, d, 2) + three + four)
 
     def total_of(kind, h):
         row0, n = bufs[kind][4:]
         value = part[z, row0 : row0 + n, toks[h]]
-        for m in (3, 2):
-            for d in (0, 1):
-                value = value + take(kind, h, d, m)
+        for got in take(kind, h, 2, 3, 4):
+            value = value + got
         tot[row0 : row0 + n, toks[h]] = value
 
     for n, (i, cp) in enumerate(loads):
@@ -246,7 +241,10 @@
     p_hl[1] = p_lo
 
     for h in (1, 0):
-        merge("kv", h)
+        merge_short("kv", h)
+    for h in (1, 0):
+        merge_long("kv", h)
+    for h in (1, 0):
         near("kv", h)
 
     spread = jnp.where(mine, gain, 0.0)
@@ -275,14 +273,17 @@
     )
 
     for h in (1, 0):
-        merge("q", h)
+        merge_short("q", h)
+    for h in (1, 0):
+        merge_long("q", h)
+    for h in (1, 0):
         near("q", h)
     lay_out(8, 16)
     decay_k = [jnp.exp(-lam * float(CL * k)) for k in range(nk)]
     block = lam * float(length)
     weight = []
-    for dy, dx, dc in moves:
-        src = place(-dy, -dx, dc)
+    for k in moves:
+        src = p ^ k
         weight.append(
             jnp.where(src < p, jnp.exp(-block * jnp.maximum(p - 1 - src, 0).astype(f32)), 0.0)
         )
@@ -294,13 +295,13 @@
             ("halo", i),
             halo_s.at[pl.ds(row0, n)],
             halo_r.at[pl.ds(row0, n)],
-            halo_ss.at[i],
+            sent.at[3],
             halo_rs.at[i],
             (after, z),
         )
 
     def tail_in(i, row0, n):
-        arrived(("halo", i), halo_r.at[pl.ds(row0, n)], halo_ss.at[i], halo_rs.at[i])
+        arrived([("halo", i)], halo_r.at[pl.ds(row0, n)], halo_rs.at[i])
 
     tail("kv", 0, 0, 2 * cs)
     total_of("kv", 0)
@@ -325,10 +326,8 @@
         carry = decay_k[1] * carry + jnp.where(mine, states[cs * k : cs * (k + 1)], 0.0)
     total = jnp.sum(carry, axis=0, keepdims=True)
     st0[...] = total
-    for i, move in enumerate(moves):
-        remote(
-            ("st", i), st0, st1.at[i], st_ss.at[i], st_rs.at[i], (place(*move), z)
-        )
+    for i, k in enumerate(moves):
+        remote(("st", i), st0, st1.at[i], sent.at[2], st_rs, (p ^ k, z))
 
     for c in range(cs):
         line = dscr[pl.ds(c, nk, stride=cs), :].astype(bf16)
@@ -340,8 +339,8 @@
     tail_in(1, 2 * cs, cs)
     query = short(2 * cs, 0)
     into = jnp.zeros((1, st), f32)
-    for i in reversed(range(len(moves))):
-        arrived(("st", i), st1.at[i], st_ss.at[i], st_rs.at[i])
+    arrived([("st", i) for i in range(len(moves))], st1, st_rs)
+    for i in range(len(moves)):
         into = into + weight[i] * st1[i]
     wide = jnp.where(mine, into, 0.0)
     x = jnp.concatenate(
@@ -366,25 +365,20 @@
         hold, step, _ = hand_on[i]
         ref = piece(i, d, hold)
         target = (p, zz(step if d == 0 else -step))
-        remote(("ag", d, i), ref, ref, ag_ss.at[d, i], ag_rs.at[d, i], target)
-
-    def handed(i, d):
-        hold, step, _ = hand_on[i]
-        arrived(("ag", d, i), piece(i, d, hold + step), ag_ss.at[d, i], ag_rs.at[d, i])
+        remote(("ag", i, d), ref, ref, sent.at[4], ag_rs.at[d if i == 0 else 2], target)
 
     for i in (0, 1):
         for d in (0, 1):
             hand(i, d)
     for d in (0, 1):
-        handed(0, d)
+        arrived([("ag", 0, d)], piece(0, d, 2), ag_rs.at[d])
         hand(2, d)
         hand(3, d)
-    for i in (1, 2, 3):
-        for d in (0, 1):
-            handed(i, d)
+    arrived([("ag", i, d) for i in (1, 2, 3) for d in (0, 1)], gath.at[pl.ds(0, 5)], ag_rs.at[2])
     out_ref[...] = gath[...]
-    for cp in sends:
-        cp.wait_send()
+    assert not pending
+    for i, ref in enumerate((kv_s, q_s, st1, halo_s, gath.at[pl.ds(0, n_ch - 1)])):
+        waiter(ref, sent.at[i]).wait_send()
 
 
 def project_kernel(w_ref, x_ref, out, rows_ref, sem):
@@ -428,10 +422,10 @@
                 pltpu.VMEM((depth, length), bf16),
                 pltpu.VMEM((rows, depth), bf16),
                 pltpu.VMEM((n_ch, per, length), f32),
-                pltpu.VMEM((2, 4, 2, 2 * cs, half), bf16),
-                pltpu.VMEM((2, 4, 2, 2 * cs, half), bf16),
-                pltpu.VMEM((2, 4, 2, cs, half), bf16),
-                pltpu.VMEM((2, 4, 2, cs, half), bf16),
+                pltpu.VMEM((2, 7, 2 * cs, half), bf16),
+                pltpu.VMEM((2, 7, 2 * cs, half), bf16),
+                pltpu.VMEM((2, 7, cs, half), bf16),
+                pltpu.VMEM((2, 7, cs, half), bf16),
                 pltpu.VMEM((per, length), f32),
                 pltpu.VMEM((per, CL), bf16),
                 pltpu.VMEM((per, CL), bf16),
@@ -447,16 +441,12 @@
                 pltpu.VMEM((nk * cs, st), f32),
                 dma((4,)),
                 dma((5,)),
-                dma((2, 4, 2)),
-                dma((2, 4, 2)),
-                dma((2, 4, 2)),
-                dma((2, 4, 2)),
+                dma((5,)),
+                dma((2, 3)),
+                dma((2, 3)),
                 dma((2,)),
-                dma((2,)),
-                dma((n_seq - 1,)),
-                dma((n_seq - 1,)),
-                dma((2, 4)),
-                dma((2, 4)),
+                dma,
+                dma((3,)),
             ],
             compiler_params=pltpu.CompilerParams(
                 collective_id=0, has_side_effects=True, vmem_limit_bytes=40 * 1024 * 1024

time: 37 us -> 35.9 us (0.970)
  the two profiles are of different devices: /device:TPU:32 before, /device:TPU:4 now
where the time goes in v4:
time: 35.9 us; the launch traced here: 35.8 us
  Pallas kernels  35.8 us (100%)
    pallas_call x1, Pallas kernels, body(): pl.pallas_call(functools.partial(conv_kernel, n_seq, n_ch), out_shape=jax...  34.2 us
    pallas_call x1, Pallas kernels, body(): pl.pallas_call(project_kernel, out_shape=jax.ShapeDtypeStruct((w_out.shap...  1.6 us

profile of v4, /device:TPU:4, one launch (start us, length us, event | category | flops | bytes accessed | tf_op | source)
XLA Modules:
  0.0 35.8 jit_solution(10829952754409486989)
XLA Ops:
  0.0 0.0 copy-start
  0.0 34.2 %shard_map.73 = bf16[8,16,1024]{2,1,0:T(8,128)(2,1)S(1)} custom-call(bf16[1024,1024]{1,0:T(8,128)(2,1)} %hid.1, bf16[1024,384]{1,0:T(8,128)(2,1)} %w_in.1, f32[3,48]{1,0:T(4,128)} %taps_in.1, f32[16,16]{1,0:T(8,128)} %rates_in.1, f32[16,16]{1,0:T(8,128)} %res_in.1, f32[1,16]{1,0:T(1,128)} %bitcast.3), custom_call_target="tpu_custom_call" | custom-call | tf_op jit(solution)/shard_map/pallas_call | solution.py:411
  34.2 0.0 copy-done
  34.2 1.6 %shard_map.74 = bf16[1024,1024]{1,0:T(8,128)(2,1)} custom-call(bf16[1024,128]{1,0:T(8,128)(2,1)S(1)} %copy-done, bf16[128,1024]{1,0:T(8,128)(2,1)S(1)} %bitcast.2), custom_call_target="tpu_custom_call" | custom-call | tf_op jit(solution)/shard_map/pallas_call | solution.py:461
Async XLA Ops:
  0.0 34.2 %copy-start = (bf16[1024,128]{1,0:T(8,128)(2,1)S(1)}, bf16[1024,128]{1,0:T(8,128)(2,1)}, u32[]{:S(2)}) copy-start(bf16[1024,128]{1,0:T(8,128)(2,1)} %w_ref.1) | copy-start | bytes 786436

commit v5 on v4

--- a/solution.py
+++ b/solution.py
@@ -13,6 +13,7 @@
 HIGH = lax.Precision.HIGHEST
 NT = (((1,), (1,)), ((), ()))
 NN = (((1,), (0,)), ((), ()))
+TN = (((0,), (0,)), ((), ()))
 CL = 128
 
 
@@ -45,7 +46,6 @@
     res_ref,
     skip_ref,
     hidv,
-    wt,
     part,
     kv_s,
     kv_r,
@@ -121,13 +121,7 @@
     for k in moves:
         pl.semaphore_signal(barrier, inc=1, device_id=(p ^ k, z), device_id_type=MESH)
 
-    new = iota((rows, rows), 0)
-    blk = (new * 1366) >> 16
-    comp = (new - blk * per) >> 4
-    old = blk * per + 3 * (new & (cs - 1)) + jnp.where(comp == 2, 0, comp + 1)
-    perm = jnp.where(old == iota((rows, rows), 1), 1.0, 0.0).astype(bf16)
     smalls[0].wait()
-    wt[...] = mm(perm, w_ref[...], NT).astype(bf16)
 
     def remote(key, src, dst, ssem, rsem, dev):
         pltpu.make_async_remote_copy(
@@ -161,10 +155,19 @@
     }
     toks = (pl.ds(0, half), pl.ds(half, half))
 
+    def rows_of(kind, dest, h):
+        comps = (1, 2) if kind == "kv" else (0,)
+        picked = []
+        for j in comps:
+            pieces = [
+                part[k, dest, pl.ds(j, cs, stride=3), :]
+                for k in range(h * nk // 2, (h + 1) * nk // 2)
+            ]
+            picked.append(jnp.concatenate(pieces, axis=1))
+        return jnp.concatenate(picked, axis=0)
+
     def own(kind, h, d, dist):
-        row0, n = bufs[kind][4:]
-        dest = zz(dist if d == 0 else -dist)
-        return part[dest, row0 : row0 + n, toks[h]]
+        return rows_of(kind, zz(dist if d == 0 else -dist), h)
 
     def long_way(h):
         return 0 if h == 1 else 1
@@ -204,7 +207,7 @@
 
     def total_of(kind, h):
         row0, n = bufs[kind][4:]
-        value = part[z, row0 : row0 + n, toks[h]]
+        value = rows_of(kind, z, h)
         for got in take(kind, h, 2, 3, 4):
             value = value + got
         tot[row0 : row0 + n, toks[h]] = value
@@ -212,7 +215,10 @@
     for n, (i, cp) in enumerate(loads):
         cp.wait()
         tok = pl.ds(i * quarter, quarter)
-        part[:, :, tok] = mm(wt[...], hidv[:, tok]).reshape(n_ch, per, quarter)
+        sums = mm(w_ref[...], hidv[:, tok], TN)
+        for k in range(quarter // CL):
+            piece = sums[:, CL * k : CL * (k + 1)].reshape(n_ch, per, CL)
+            part[i * quarter // CL + k] = piece
         if n == 1:
             pl.semaphore_wait(barrier, 4 + len(moves))
             far("kv", 1)
@@ -234,11 +240,12 @@
     gain = as_row(res_ref[...] * jnp.sqrt(rates_ref[...]))
     steps = iota((CL, st), 0).astype(f32)
     e_hi, e_lo = halves(jnp.exp(-lam * (CL - 1 - steps)))
-    e_hl[0] = e_hi
-    e_hl[1] = e_lo
+    e_hl[0:CL] = e_hi
+    e_hl[CL : 2 * CL] = e_lo
     p_hi, p_lo = halves(gain * jnp.exp(-lam * (steps + 1.0)))
-    p_hl[0] = p_hi
-    p_hl[1] = p_lo
+    p_hl[:, 0:st] = p_hi
+    p_hl[:, st : 2 * st] = p_hi
+    p_hl[:, 2 * st : 3 * st] = p_lo
 
     for h in (1, 0):
         merge_short("kv", h)
@@ -278,6 +285,7 @@
         merge_long("q", h)
     for h in (1, 0):
         near("q", h)
+
     lay_out(8, 16)
     decay_k = [jnp.exp(-lam * float(CL * k)) for k in range(nk)]
     block = lam * float(length)
@@ -287,6 +295,7 @@
         weight.append(
             jnp.where(src < p, jnp.exp(-block * jnp.maximum(p - 1 - src, 0).astype(f32)), 0.0)
         )
+
     total_of("kv", 1)
 
     def tail(kind, i, row0, n):
@@ -316,10 +325,11 @@
         return t[0] * x + t[1] * one + t[2] * two
 
     tail_in(0, 0, 2 * cs)
+
     driven = (short(0, 1) * short(cs, 2)).astype(bf16)
     stacked = jnp.concatenate([driven[:, CL * k : CL * (k + 1)] for k in range(nk)], axis=0)
     dscr[...] = stacked.astype(f32)
-    states = mm(stacked, e_hl[0]) + mm(stacked, e_hl[1])
+    states = mm(jnp.concatenate([stacked, stacked], axis=1), e_hl[...])
     carry = jnp.zeros((cs, st), f32)
     for k in range(nk):
         xscr[cs * k : cs * (k + 1)] = carry
@@ -329,32 +339,36 @@
     for i, k in enumerate(moves):
         remote(("st", i), st0, st1.at[i], sent.at[2], st_rs, (p ^ k, z))
 
+    total_of("q", 1)
+    tail("q", 1, 2 * cs, cs)
+    total_of("q", 0)
+
     for c in range(cs):
         line = dscr[pl.ds(c, nk, stride=cs), :].astype(bf16)
         yscr[pl.ds(c, nk, stride=cs), :] = mm(jnp.concatenate([line, line], axis=1), tcat[c])
 
-    total_of("q", 1)
-    tail("q", 1, 2 * cs, cs)
-    total_of("q", 0)
     tail_in(1, 2 * cs, cs)
     query = short(2 * cs, 0)
-    into = jnp.zeros((1, st), f32)
+
     arrived([("st", i) for i in range(len(moves))], st1, st_rs)
-    for i in range(len(moves)):
-        into = into + weight[i] * st1[i]
+    terms = [weight[i] * st1[i] for i in range(len(moves))]
+    while len(terms) > 1:
+        terms = [sum(terms[i : i + 2]) for i in range(0, len(terms), 2)]
+    into = terms[0]
+
     wide = jnp.where(mine, into, 0.0)
     x = jnp.concatenate(
         [xscr[cs * k : cs * (k + 1)] + decay_k[k] * wide for k in range(nk)], axis=0
     )
     x_hi, x_lo = halves(x)
-    y = yscr[...] + mm(x_hi, p_hl[0], NT) + mm(x_lo, p_hl[0], NT) + mm(x_hi, p_hl[1], NT)
+    y = yscr[...] + mm(jnp.concatenate([x_hi, x_lo, x_hi], axis=1), p_hl[...], NT)
     for k in range(nk):
         sl = slice(cs * k, cs * (k + 1))
         tok = slice(CL * k, CL * (k + 1))
         value = query[:, tok] * (y[sl] + skip_col * dscr[sl])
         gath[z, :, tok] = value.astype(bf16)
 
-    hand_on = ((0, 2, None), (0, 1, None), (2, 1, None), (2, 2, 0))
+    hand_on = ((0, 2, 0), (0, 2, 1), (0, 1, None), (2, 2, 0), (2, 1, 0), (2, 1, 1))
 
     def piece(i, d, dist):
         part_of = hand_on[i][2]
@@ -365,17 +379,20 @@
         hold, step, _ = hand_on[i]
         ref = piece(i, d, hold)
         target = (p, zz(step if d == 0 else -step))
-        remote(("ag", i, d), ref, ref, sent.at[4], ag_rs.at[d if i == 0 else 2], target)
-
+        remote(("ag", i, d), ref, ref, sent.at[4], ag_rs.at[2 * i + d if i < 2 else 4], target)
+
+    for i in (0, 1, 2):
+        for d in (0, 1):
+            hand(i, d)
     for i in (0, 1):
         for d in (0, 1):
-            hand(i, d)
-    for d in (0, 1):
-        arrived([("ag", 0, d)], piece(0, d, 2), ag_rs.at[d])
-        hand(2, d)
-        hand(3, d)
-    arrived([("ag", i, d) for i in (1, 2, 3) for d in (0, 1)], gath.at[pl.ds(0, 5)], ag_rs.at[2])
+            arrived([("ag", i, d)], piece(i, d, 2), ag_rs.at[2 * i + d])
+            if i == 0:
+                hand(3, d)
+            hand(4 + i, d)
+    arrived([("ag", i, d) for i in range(2, 6) for d in (0, 1)], gath.at[pl.ds(0, 5)], ag_rs.at[4])
     out_ref[...] = gath[...]
+
     assert not pending
     for i, ref in enumerate((kv_s, q_s, st1, halo_s, gath.at[pl.ds(0, n_ch - 1)])):
         waiter(ref, sent.at[i]).wait_send()
@@ -420,8 +437,7 @@
                 pltpu.VMEM(residues.shape, f32),
                 pltpu.VMEM((1, cs), f32),
                 pltpu.VMEM((depth, length), bf16),
-                pltpu.VMEM((rows, depth), bf16),
-                pltpu.VMEM((n_ch, per, length), f32),
+                pltpu.VMEM((nk, n_ch, per, CL), f32),
                 pltpu.VMEM((2, 7, 2 * cs, half), bf16),
                 pltpu.VMEM((2, 7, 2 * cs, half), bf16),
                 pltpu.VMEM((2, 7, cs, half), bf16),
@@ -433,8 +449,8 @@
                 pltpu.VMEM((1, st), f32),
                 pltpu.VMEM((n_seq - 1, 1, st), f32),
                 pltpu.VMEM((9, cs, CL), f32),
-                pltpu.VMEM((2, CL, st), bf16),
-                pltpu.VMEM((2, CL, st), bf16),
+                pltpu.VMEM((2 * CL, st), bf16),
+                pltpu.VMEM((CL, 3 * st), bf16),
                 pltpu.VMEM((cs, 2 * CL, CL), bf16),
                 pltpu.VMEM((nk * cs, CL), f32),
                 pltpu.VMEM((nk * cs, CL), f32),
@@ -446,7 +462,7 @@
                 dma((2, 3)),
                 dma((2,)),
                 dma,
-                dma((3,)),
+                dma((5,)),
             ],
             compiler_params=pltpu.CompilerParams(
                 collective_id=0, has_side_effects=True, vmem_limit_bytes=40 * 1024 * 1024

time: 35.9 us -> 35.5 us (0.989)
  the two profiles are of different devices: /device:TPU:4 before, /device:TPU:24 now
where the time goes in v5:
time: 35.5 us; the launch traced here: 35 us
  Pallas kernels  35 us (99%)
    pallas_call x1, Pallas kernels, body(): pl.pallas_call(functools.partial(conv_kernel, n_seq, n_ch), out_shape=jax...  33.4 us
    pallas_call x1, Pallas kernels, body(): pl.pallas_call(project_kernel, out_shape=jax.ShapeDtypeStruct((w_out.shap...  1.59 us

profile of v5, /device:TPU:24, one launch (start us, length us, event | category | flops | bytes accessed | tf_op | source)
XLA Modules:
  0.0 35.0 jit_solution(18393402968852655619)
XLA Ops:
  0.0 0.0 copy-start
  0.0 33.4 %shard_map.73 = bf16[8,16,1024]{2,1,0:T(8,128)(2,1)S(1)} custom-call(bf16[1024,1024]{1,0:T(8,128)(2,1)} %hid.1, bf16[1024,384]{1,0:T(8,128)(2,1)} %w_in.1, f32[3,48]{1,0:T(4,128)} %taps_in.1, f32[16,16]{1,0:T(8,128)} %rates_in.1, f32[16,16]{1,0:T(8,128)} %res_in.1, f32[1,16]{1,0:T(1,128)} %bitcast.3), custom_call_target="tpu_custom_call" | custom-call | tf_op jit(solution)/shard_map/pallas_call | solution.py:428
  33.4 0.0 copy-done
  33.4 1.6 %shard_map.74 = bf16[1024,1024]{1,0:T(8,128)(2,1)} custom-call(bf16[1024,128]{1,0:T(8,128)(2,1)S(1)} %copy-done, bf16[128,1024]{1,0:T(8,128)(2,1)S(1)} %bitcast.2), custom_call_target="tpu_custom_call" | custom-call | tf_op jit(solution)/shard_map/pallas_call | solution.py:477
Async XLA Ops:
  0.0 33.4 %copy-start = (bf16[1024,128]{1,0:T(8,128)(2,1)S(1)}, bf16[1024,128]{1,0:T(8,128)(2,1)}, u32[]{:S(2)}) copy-start(bf16[1024,128]{1,0:T(8,128)(2,1)} %w_ref.1) | copy-start | bytes 786436

commit v6 on v5

--- a/solution.py
+++ b/solution.py
@@ -57,6 +57,8 @@
     gath,
     st0,
     st1,
+    weight,
+    into,
     par,
     e_hl,
     p_hl,
@@ -70,7 +72,9 @@
     kv_rs,
     q_rs,
     halo_rs,
+    st_ss,
     st_rs,
+    ready,
     ag_rs,
 ):
     p = lax.axis_index("seq")
@@ -113,13 +117,25 @@
     def hops(k):
         return (0, 1, 2, 1)[k >> 1 & 3] + (0, 1, 2, 1)[k >> 3]
 
-    moves = sorted(range(1, n_seq), key=lambda k: -hops(k))
+    bits = n_seq.bit_length() - 1
+    groups = [sorted(range(1 << b, 2 << b), key=lambda k: -hops(k)) for b in range(bits)]
+
+    def to_later(b):
+        return pl.when((p >> b) & 1 == 0)
+
+    def to_earlier(b):
+        return pl.when((p >> b) & 1 == 1)
+
     after = lax.rem(p + 1, n_seq)
     barrier = pltpu.get_barrier_semaphore()
     for s in ring + ring2:
         pl.semaphore_signal(barrier, inc=1, device_id=(p, s), device_id_type=MESH)
-    for k in moves:
-        pl.semaphore_signal(barrier, inc=1, device_id=(p ^ k, z), device_id_type=MESH)
+    for b in reversed(range(bits)):
+
+        @to_later(b)
+        def _():
+            for k in groups[b]:
+                pl.semaphore_signal(barrier, inc=1, device_id=(p ^ k, z), device_id_type=MESH)
 
     smalls[0].wait()
 
@@ -220,12 +236,22 @@
             piece = sums[:, CL * k : CL * (k + 1)].reshape(n_ch, per, CL)
             part[i * quarter // CL + k] = piece
         if n == 1:
-            pl.semaphore_wait(barrier, 4 + len(moves))
+            pl.semaphore_wait(barrier, 4 + p)
             far("kv", 1)
         if n == 3:
             far("kv", 0)
             far("q", 1)
             far("q", 0)
+    for b in reversed(range(bits)):
+
+        @to_earlier(b)
+        def _():
+            for k in groups[b]:
+                pl.semaphore_signal(ready, inc=1, device_id=(p ^ k, z), device_id_type=MESH)
+
+    @pl.when(p == 0)
+    def _():
+        halo_r[...] = jnp.zeros_like(halo_r)
 
     lane_st = iota((cs, st), 1)
     mine = (lane_st >> 4) == iota((cs, st), 0)
@@ -285,38 +311,38 @@
         merge_long("q", h)
     for h in (1, 0):
         near("q", h)
-
     lay_out(8, 16)
     decay_k = [jnp.exp(-lam * float(CL * k)) for k in range(nk)]
     block = lam * float(length)
-    weight = []
-    for k in moves:
-        src = p ^ k
-        weight.append(
-            jnp.where(src < p, jnp.exp(-block * jnp.maximum(p - 1 - src, 0).astype(f32)), 0.0)
-        )
-
+    for k in range(1, n_seq):
+        apart = jnp.maximum(p - 1 - (p ^ k), 0)
+        weight[k] = jnp.exp(-block * apart.astype(f32))
     total_of("kv", 1)
 
-    def tail(kind, i, row0, n):
+    def tail(i, row0, n):
         halo_s[row0 : row0 + n] = tot[row0 : row0 + n, length - CL : length].astype(bf16)
-        remote(
-            ("halo", i),
-            halo_s.at[pl.ds(row0, n)],
-            halo_r.at[pl.ds(row0, n)],
-            sent.at[3],
-            halo_rs.at[i],
-            (after, z),
-        )
+        at = pl.ds(row0, n)
+
+        @pl.when(p < n_seq - 1)
+        def _():
+            remote(
+                ("halo", i), halo_s.at[at], halo_r.at[at], sent.at[2], halo_rs.at[i], (after, z)
+            )
 
     def tail_in(i, row0, n):
-        arrived([("halo", i)], halo_r.at[pl.ds(row0, n)], halo_rs.at[i])
-
-    tail("kv", 0, 0, 2 * cs)
+        @pl.when(p > 0)
+        def _():
+            arrived([("halo", i)], halo_r.at[pl.ds(row0, n)], halo_rs.at[i])
+
+    @pl.when(p < n_seq - 1)
+    def _():
+        pl.semaphore_wait(ready, n_seq - 1 - p)
+
+    tail(0, 0, 2 * cs)
     total_of("kv", 0)
 
     def short(row0, j):
-        edge = jnp.where(p > 0, halo_r[row0 : row0 + cs].astype(f32), 0.0)
+        edge = halo_r[row0 : row0 + cs].astype(f32)
         x = tot[row0 : row0 + cs]
         ext = jnp.concatenate([edge, x], axis=1)
         one = pltpu.roll(ext, 1, 1)[:, CL:]
@@ -325,7 +351,6 @@
         return t[0] * x + t[1] * one + t[2] * two
 
     tail_in(0, 0, 2 * cs)
-
     driven = (short(0, 1) * short(cs, 2)).astype(bf16)
     stacked = jnp.concatenate([driven[:, CL * k : CL * (k + 1)] for k in range(nk)], axis=0)
     dscr[...] = stacked.astype(f32)
@@ -336,27 +361,32 @@
         carry = decay_k[1] * carry + jnp.where(mine, states[cs * k : cs * (k + 1)], 0.0)
     total = jnp.sum(carry, axis=0, keepdims=True)
     st0[...] = total
-    for i, k in enumerate(moves):
-        remote(("st", i), st0, st1.at[i], sent.at[2], st_rs, (p ^ k, z))
+    for b in reversed(range(bits)):
+
+        @to_later(b)
+        def _():
+            for k in groups[b]:
+                remote(("st", k), st0, st1.at[k], st_ss.at[b], st_rs.at[b], (p ^ k, z))
 
     total_of("q", 1)
-    tail("q", 1, 2 * cs, cs)
+    tail(1, 2 * cs, cs)
     total_of("q", 0)
-
     for c in range(cs):
         line = dscr[pl.ds(c, nk, stride=cs), :].astype(bf16)
         yscr[pl.ds(c, nk, stride=cs), :] = mm(jnp.concatenate([line, line], axis=1), tcat[c])
 
     tail_in(1, 2 * cs, cs)
     query = short(2 * cs, 0)
-
-    arrived([("st", i) for i in range(len(moves))], st1, st_rs)
-    terms = [weight[i] * st1[i] for i in range(len(moves))]
-    while len(terms) > 1:
-        terms = [sum(terms[i : i + 2]) for i in range(0, len(terms), 2)]
-    into = terms[0]
-
-    wide = jnp.where(mine, into, 0.0)
+    into[...] = jnp.zeros_like(into)
+    for b in reversed(range(bits)):
+
+        @to_earlier(b)
+        def _():
+            group = pl.ds(1 << b, 1 << b)
+            arrived([("st", k) for k in groups[b]], st1.at[group], st_rs.at[b])
+            into[...] += jnp.sum(weight[group] * st1[group], axis=0)
+
+    wide = jnp.where(mine, into[...], 0.0)
     x = jnp.concatenate(
         [xscr[cs * k : cs * (k + 1)] + decay_k[k] * wide for k in range(nk)], axis=0
     )
@@ -379,7 +409,7 @@
         hold, step, _ = hand_on[i]
         ref = piece(i, d, hold)
         target = (p, zz(step if d == 0 else -step))
-        remote(("ag", i, d), ref, ref, sent.at[4], ag_rs.at[2 * i + d if i < 2 else 4], target)
+        remote(("ag", i, d), ref, ref, sent.at[3], ag_rs.at[2 * i + d if i < 2 else 4], target)
 
     for i in (0, 1, 2):
         for d in (0, 1):
@@ -392,10 +422,19 @@
             hand(4 + i, d)
     arrived([("ag", i, d) for i in range(2, 6) for d in (0, 1)], gath.at[pl.ds(0, 5)], ag_rs.at[4])
     out_ref[...] = gath[...]
-
     assert not pending
-    for i, ref in enumerate((kv_s, q_s, st1, halo_s, gath.at[pl.ds(0, n_ch - 1)])):
+    for i, ref in ((0, kv_s), (1, q_s), (3, gath.at[pl.ds(0, n_ch - 1)])):
         waiter(ref, sent.at[i]).wait_send()
+
+    @pl.when(p < n_seq - 1)
+    def _():
+        waiter(halo_s, sent.at[2]).wait_send()
+
+    for b in range(bits):
+
+        @to_later(b)
+        def _():
+            waiter(st1.at[pl.ds(1 << b, 1 << b)], st_ss.at[b]).wait_send()
 
 
 def project_kernel(w_ref, x_ref, out, rows_ref, sem):
@@ -423,6 +462,7 @@
         st = cs * rates.shape[1]
         half = length // 2
         nk = length // CL
+        bits = n_seq.bit_length() - 1
         vmem = pl.BlockSpec(memory_space=pltpu.VMEM)
         dma = pltpu.SemaphoreType.DMA
         gathered = pl.pallas_call(
@@ -447,7 +487,9 @@
                 pltpu.VMEM((per, CL), bf16),
                 pltpu.VMEM((n_ch, cs, length), bf16),
                 pltpu.VMEM((1, st), f32),
-                pltpu.VMEM((n_seq - 1, 1, st), f32),
+                pltpu.VMEM((n_seq, 1, st), f32),
+                pltpu.VMEM((n_seq, 1, st), f32),
+                pltpu.VMEM((1, st), f32),
                 pltpu.VMEM((9, cs, CL), f32),
                 pltpu.VMEM((2 * CL, st), bf16),
                 pltpu.VMEM((CL, 3 * st), bf16),
@@ -457,11 +499,13 @@
                 pltpu.VMEM((nk * cs, st), f32),
                 dma((4,)),
                 dma((5,)),
-                dma((5,)),
+                dma((4,)),
                 dma((2, 3)),
                 dma((2, 3)),
                 dma((2,)),
-                dma,
+                dma((bits,)),
+                dma((bits,)),
+                pltpu.SemaphoreType.REGULAR,
                 dma((5,)),
             ],
             compiler_params=pltpu.CompilerParams(

time: 35.5 us -> 34.3 us (0.966); the launches traced: 35 us -> 34.2 us
  Pallas kernels: 35 us -> 34.2 us
    pallas_call x1, Pallas kernels: 33.4 us -> 32.6 us  [body(): pl.pallas_call(functools.partial(conv_kernel, n_seq, n_ch), out_shape=jax...]
where the time goes in v6:
time: 34.3 us; the launch traced here: 34.2 us
  Pallas kernels  34.2 us (100%)
    pallas_call x1, Pallas kernels, body(): pl.pallas_call(functools.partial(conv_kernel, n_seq, n_ch), out_shape=jax...  32.6 us
    pallas_call x1, Pallas kernels, body(): pl.pallas_call(project_kernel, out_shape=jax.ShapeDtypeStruct((w_out.shap...  1.59 us

profile of v6, /device:TPU:24, one launch (start us, length us, event | category | flops | bytes accessed | tf_op | source)
XLA Modules:
  0.0 34.2 jit_solution(807504520957311398)
XLA Ops:
  0.0 0.0 copy-start
  0.0 32.6 %shard_map.73 = bf16[8,16,1024]{2,1,0:T(8,128)(2,1)S(1)} custom-call(bf16[1024,1024]{1,0:T(8,128)(2,1)} %hid.1, bf16[1024,384]{1,0:T(8,128)(2,1)} %w_in.1, f32[3,48]{1,0:T(4,128)} %taps_in.1, f32[16,16]{1,0:T(8,128)} %rates_in.1, f32[16,16]{1,0:T(8,128)} %res_in.1, f32[1,16]{1,0:T(1,128)} %bitcast.3), custom_call_target="tpu_custom_call" | custom-call | tf_op jit(solution)/shard_map/pallas_call | solution.py:468
  32.6 0.0 copy-done
  32.6 1.6 %shard_map.74 = bf16[1024,1024]{1,0:T(8,128)(2,1)} custom-call(bf16[1024,128]{1,0:T(8,128)(2,1)S(1)} %copy-done, bf16[128,1024]{1,0:T(8,128)(2,1)S(1)} %bitcast.2), custom_call_target="tpu_custom_call" | custom-call | tf_op jit(solution)/shard_map/pallas_call | solution.py:521
Async XLA Ops:
  0.0 32.6 %copy-start = (bf16[1024,128]{1,0:T(8,128)(2,1)S(1)}, bf16[1024,128]{1,0:T(8,128)(2,1)}, u32[]{:S(2)}) copy-start(bf16[1024,128]{1,0:T(8,128)(2,1)} %w_ref.1) | copy-start | bytes 786436

commit v7 on v6

--- a/solution.py
+++ b/solution.py
@@ -128,7 +128,7 @@
 
     after = lax.rem(p + 1, n_seq)
     barrier = pltpu.get_barrier_semaphore()
-    for s in ring + ring2:
+    for s in [zz(k) for k in (1, 2, 3, 5, 6, 7)]:
         pl.semaphore_signal(barrier, inc=1, device_id=(p, s), device_id_type=MESH)
     for b in reversed(range(bits)):
 
@@ -236,7 +236,7 @@
             piece = sums[:, CL * k : CL * (k + 1)].reshape(n_ch, per, CL)
             part[i * quarter // CL + k] = piece
         if n == 1:
-            pl.semaphore_wait(barrier, 4 + p)
+            pl.semaphore_wait(barrier, 6 + p)
             far("kv", 1)
         if n == 3:
             far("kv", 0)
@@ -398,29 +398,44 @@
         value = query[:, tok] * (y[sl] + skip_col * dscr[sl])
         gath[z, :, tok] = value.astype(bf16)
 
-    hand_on = ((0, 2, 0), (0, 2, 1), (0, 1, None), (2, 2, 0), (2, 1, 0), (2, 1, 1))
-
-    def piece(i, d, dist):
-        part_of = hand_on[i][2]
-        tok = slice(None) if part_of is None else toks[part_of if d == 0 else 1 - part_of]
+    def piece(move, d, dist):
+        tok = slice(None) if move[2] is None else toks[move[2] if d == 0 else 1 - move[2]]
         return gath.at[zz(-dist if d == 0 else dist), :, tok]
 
-    def hand(i, d):
-        hold, step, _ = hand_on[i]
-        ref = piece(i, d, hold)
-        target = (p, zz(step if d == 0 else -step))
-        remote(("ag", i, d), ref, ref, sent.at[3], ag_rs.at[2 * i + d if i < 2 else 4], target)
-
-    for i in (0, 1, 2):
+    def hand(move, d, sem):
+        ref = piece(move, d, move[0])
+        target = (p, zz(move[1] if d == 0 else -move[1]))
+        remote(("ag", move, d), ref, ref, sent.at[3], ag_rs.at[sem], target)
+
+    def handed(moves, d, sem, ref):
+        arrived([("ag", move, way) for move in moves for way in d], ref, ag_rs.at[sem])
+
+    def straight():
+        plan = ((0, 3, 0), (0, 1, None), (0, 2, None), (0, 3, 1))
+        last = (3, 1, 0)
+        for i, move in enumerate(plan):
+            for d in (0, 1):
+                hand(move, d, d if i == 0 else 4)
         for d in (0, 1):
-            hand(i, d)
-    for i in (0, 1):
-        for d in (0, 1):
-            arrived([("ag", i, d)], piece(i, d, 2), ag_rs.at[2 * i + d])
-            if i == 0:
-                hand(3, d)
-            hand(4 + i, d)
-    arrived([("ag", i, d) for i in range(2, 6) for d in (0, 1)], gath.at[pl.ds(0, 5)], ag_rs.at[4])
+            handed([plan[0]], (d,), d, piece(plan[0], d, 3))
+            hand(last, d, 4)
+        handed(plan[1:] + (last,), (0, 1), 4, gath.at[pl.ds(0, n_ch - 2)])
+
+    def relayed():
+        plan = ((0, 2, 0), (0, 2, 1), (0, 1, None), (2, 2, 0), (2, 1, 0), (2, 1, 1))
+        for i, move in enumerate(plan[:3]):
+            for d in (0, 1):
+                hand(move, d, 2 * i + d if i < 2 else 4)
+        for i in (0, 1):
+            for d in (0, 1):
+                handed([plan[i]], (d,), 2 * i + d, piece(plan[i], d, 2))
+                if i == 0:
+                    hand(plan[3], d, 4)
+                hand(plan[4 + i], d, 4)
+        handed(plan[2:], (0, 1), 4, gath.at[pl.ds(0, n_ch - 3)])
+
+    pl.when(p % 2 == 0)(straight)
+    pl.when(p % 2 == 1)(relayed)
     out_ref[...] = gath[...]
     assert not pending
     for i, ref in ((0, kv_s), (1, q_s), (3, gath.at[pl.ds(0, n_ch - 1)])):

time: 34.3 us -> 33.6 us (0.980)
  Pallas kernels: 34.2 us -> 33.5 us
    pallas_call x1, Pallas kernels: 32.6 us -> 31.9 us  [body(): pl.pallas_call(functools.partial(conv_kernel, n_seq, n_ch), out_shape=jax...]
where the time goes in v7:
time: 33.6 us
  Pallas kernels  33.5 us (100%)
    pallas_call x1, Pallas kernels, body(): pl.pallas_call(functools.partial(conv_kernel, n_seq, n_ch), out_shape=jax...  31.9 us
    pallas_call x1, Pallas kernels, body(): pl.pallas_call(project_kernel, out_shape=jax.ShapeDtypeStruct((w_out.shap...  1.6 us

profile of v7, /device:TPU:24, one launch (start us, length us, event | category | flops | bytes accessed | tf_op | source)
XLA Modules:
  0.0 33.6 jit_solution(4619219097890849900)
XLA Ops:
  0.0 0.0 copy-start
  0.0 31.9 %shard_map.73 = bf16[8,16,1024]{2,1,0:T(8,128)(2,1)S(1)} custom-call(bf16[1024,1024]{1,0:T(8,128)(2,1)} %hid.1, bf16[1024,384]{1,0:T(8,128)(2,1)} %w_in.1, f32[3,48]{1,0:T(4,128)} %taps_in.1, f32[16,16]{1,0:T(8,128)} %rates_in.1, f32[16,16]{1,0:T(8,128)} %res_in.1, f32[1,16]{1,0:T(1,128)} %bitcast.3), custom_call_target="tpu_custom_call" | custom-call | tf_op jit(solution)/shard_map/pallas_call | solution.py:483
  32.0 0.0 copy-done
  32.0 1.6 %shard_map.74 = bf16[1024,1024]{1,0:T(8,128)(2,1)} custom-call(bf16[1024,128]{1,0:T(8,128)(2,1)S(1)} %copy-done, bf16[128,1024]{1,0:T(8,128)(2,1)S(1)} %bitcast.2), custom_call_target="tpu_custom_call" | custom-call | tf_op jit(solution)/shard_map/pallas_call | solution.py:536
Async XLA Ops:
  0.0 32.0 %copy-start = (bf16[1024,128]{1,0:T(8,128)(2,1)S(1)}, bf16[1024,128]{1,0:T(8,128)(2,1)}, u32[]{:S(2)}) copy-start(bf16[1024,128]{1,0:T(8,128)(2,1)} %w_ref.1) | copy-start | bytes 786436

commit v8 on v7

--- a/solution.py
+++ b/solution.py
@@ -306,11 +306,11 @@
     )
 
     for h in (1, 0):
+        near("q", h)
+    for h in (1, 0):
         merge_short("q", h)
     for h in (1, 0):
         merge_long("q", h)
-    for h in (1, 0):
-        near("q", h)
     lay_out(8, 16)
     decay_k = [jnp.exp(-lam * float(CL * k)) for k in range(nk)]
     block = lam * float(length)

time: 33.6 us -> 33.7 us (level)
  no operation moved by 1% of the time
where the time goes in v8:
time: 33.7 us; the launch traced here: 33.6 us
  Pallas kernels  33.6 us (100%)
    pallas_call x1, Pallas kernels, body(): pl.pallas_call(functools.partial(conv_kernel, n_seq, n_ch), out_shape=jax...  32 us
    pallas_call x1, Pallas kernels, body(): pl.pallas_call(project_kernel, out_shape=jax.ShapeDtypeStruct((w_out.shap...  1.6 us

profile of v8, /device:TPU:24, one launch (start us, length us, event | category | flops | bytes accessed | tf_op | source)
XLA Modules:
  0.0 33.6 jit_solution(723149988227286834)
XLA Ops:
  0.0 0.0 copy-start
  0.0 32.0 %shard_map.73 = bf16[8,16,1024]{2,1,0:T(8,128)(2,1)S(1)} custom-call(bf16[1024,1024]{1,0:T(8,128)(2,1)} %hid.1, bf16[1024,384]{1,0:T(8,128)(2,1)} %w_in.1, f32[3,48]{1,0:T(4,128)} %taps_in.1, f32[16,16]{1,0:T(8,128)} %rates_in.1, f32[16,16]{1,0:T(8,128)} %res_in.1, f32[1,16]{1,0:T(1,128)} %bitcast.3), custom_call_target="tpu_custom_call" | custom-call | tf_op jit(solution)/shard_map/pallas_call | solution.py:483
  32.0 0.0 copy-done
  32.0 1.6 %shard_map.74 = bf16[1024,1024]{1,0:T(8,128)(2,1)} custom-call(bf16[1024,128]{1,0:T(8,128)(2,1)S(1)} %copy-done, bf16[128,1024]{1,0:T(8,128)(2,1)S(1)} %bitcast.2), custom_call_target="tpu_custom_call" | custom-call | tf_op jit(solution)/shard_map/pallas_call | solution.py:536
Async XLA Ops:
  0.0 32.0 %copy-start = (bf16[1024,128]{1,0:T(8,128)(2,1)S(1)}, bf16[1024,128]{1,0:T(8,128)(2,1)}, u32[]{:S(2)}) copy-start(bf16[1024,128]{1,0:T(8,128)(2,1)} %w_ref.1) | copy-start | bytes 786436

commit v9 on v8

--- a/solution.py
+++ b/solution.py
@@ -341,25 +341,37 @@
     tail(0, 0, 2 * cs)
     total_of("kv", 0)
 
-    def short(row0, j):
+    def short(row0, j, count):
         edge = halo_r[row0 : row0 + cs].astype(f32)
-        x = tot[row0 : row0 + cs]
+        x = tot[row0 : row0 + cs, 0:count]
         ext = jnp.concatenate([edge, x], axis=1)
         one = pltpu.roll(ext, 1, 1)[:, CL:]
         two = pltpu.roll(ext, 2, 1)[:, CL:]
         t = [par[3 * i + j][:, 0:1] for i in range(3)]
         return t[0] * x + t[1] * one + t[2] * two
 
+    def inner(row0, j):
+        x = tot[row0 : row0 + cs]
+        one, two = pltpu.roll(x, 1, 1), pltpu.roll(x, 2, 1)
+        t = [par[3 * i + j][:, 0:1] for i in range(3)]
+        return (t[0] * x + t[1] * one + t[2] * two)[:, CL:]
+
+    def states_of(rows_bf):
+        return mm(jnp.concatenate([rows_bf, rows_bf], axis=1), e_hl[...])
+
+    later = (inner(0, 1) * inner(cs, 2)).astype(bf16)
+    stacked = jnp.concatenate([later[:, CL * k : CL * (k + 1)] for k in range(nk - 1)], axis=0)
+    dscr[cs:] = stacked.astype(f32)
+    states = states_of(stacked)
+    carry = jnp.zeros((cs, st), f32)
+    for k in range(1, nk):
+        xscr[cs * k : cs * (k + 1)] = carry
+        carry = decay_k[1] * carry + jnp.where(mine, states[cs * (k - 1) : cs * k], 0.0)
+
     tail_in(0, 0, 2 * cs)
-    driven = (short(0, 1) * short(cs, 2)).astype(bf16)
-    stacked = jnp.concatenate([driven[:, CL * k : CL * (k + 1)] for k in range(nk)], axis=0)
-    dscr[...] = stacked.astype(f32)
-    states = mm(jnp.concatenate([stacked, stacked], axis=1), e_hl[...])
-    carry = jnp.zeros((cs, st), f32)
-    for k in range(nk):
-        xscr[cs * k : cs * (k + 1)] = carry
-        carry = decay_k[1] * carry + jnp.where(mine, states[cs * k : cs * (k + 1)], 0.0)
-    total = jnp.sum(carry, axis=0, keepdims=True)
+    leading = (short(0, 1, CL) * short(cs, 2, CL)).astype(bf16)
+    entry = jnp.where(mine, states_of(leading), 0.0)
+    total = jnp.sum(carry + decay_k[nk - 1] * entry, axis=0, keepdims=True)
     st0[...] = total
     for b in reversed(range(bits)):
 
@@ -368,6 +380,10 @@
             for k in groups[b]:
                 remote(("st", k), st0, st1.at[k], st_ss.at[b], st_rs.at[b], (p ^ k, z))
 
+    dscr[0:cs] = leading.astype(f32)
+    xscr[0:cs] = jnp.zeros((cs, st), f32)
+    for k in range(1, nk):
+        xscr[cs * k : cs * (k + 1)] += decay_k[k - 1] * entry
     total_of("q", 1)
     tail(1, 2 * cs, cs)
     total_of("q", 0)
@@ -376,7 +392,7 @@
         yscr[pl.ds(c, nk, stride=cs), :] = mm(jnp.concatenate([line, line], axis=1), tcat[c])
 
     tail_in(1, 2 * cs, cs)
-    query = short(2 * cs, 0)
+    query = short(2 * cs, 0, length)
     into[...] = jnp.zeros_like(into)
     for b in reversed(range(bits)):
 

time: 33.7 us -> 33.9 us (level)
  no operation moved by 1% of the time
where the time goes in v9:
time: 33.9 us; the launch traced here: 33.8 us
  Pallas kernels  33.8 us (100%)
    pallas_call x1, Pallas kernels, body(): pl.pallas_call(functools.partial(conv_kernel, n_seq, n_ch), out_shape=jax...  32.2 us
    pallas_call x1, Pallas kernels, body(): pl.pallas_call(project_kernel, out_shape=jax.ShapeDtypeStruct((w_out.shap...  1.6 us

profile of v9, /device:TPU:24, one launch (start us, length us, event | category | flops | bytes accessed | tf_op | source)
XLA Modules:
  0.0 33.8 jit_solution(8546951321453846647)
XLA Ops:
  0.0 0.0 copy-start
  0.0 32.2 %shard_map.73 = bf16[8,16,1024]{2,1,0:T(8,128)(2,1)S(1)} custom-call(bf16[1024,1024]{1,0:T(8,128)(2,1)} %hid.1, bf16[1024,384]{1,0:T(8,128)(2,1)} %w_in.1, f32[3,48]{1,0:T(4,128)} %taps_in.1, f32[16,16]{1,0:T(8,128)} %rates_in.1, f32[16,16]{1,0:T(8,128)} %res_in.1, f32[1,16]{1,0:T(1,128)} %bitcast.3), custom_call_target="tpu_custom_call" | custom-call | tf_op jit(solution)/shard_map/pallas_call | solution.py:499
  32.2 0.0 copy-done
  32.2 1.6 %shard_map.74 = bf16[1024,1024]{1,0:T(8,128)(2,1)} custom-call(bf16[1024,128]{1,0:T(8,128)(2,1)S(1)} %copy-done, bf16[128,1024]{1,0:T(8,128)(2,1)S(1)} %bitcast.2), custom_call_target="tpu_custom_call" | custom-call | tf_op jit(solution)/shard_map/pallas_call | solution.py:552
Async XLA Ops:
  0.0 32.2 %copy-start = (bf16[1024,128]{1,0:T(8,128)(2,1)S(1)}, bf16[1024,128]{1,0:T(8,128)(2,1)}, u32[]{:S(2)}) copy-start(bf16[1024,128]{1,0:T(8,128)(2,1)} %w_ref.1) | copy-start | bytes 786436

commit v10 on v9

--- a/solution.py
+++ b/solution.py
@@ -268,10 +268,10 @@
     e_hi, e_lo = halves(jnp.exp(-lam * (CL - 1 - steps)))
     e_hl[0:CL] = e_hi
     e_hl[CL : 2 * CL] = e_lo
-    p_hi, p_lo = halves(gain * jnp.exp(-lam * (steps + 1.0)))
-    p_hl[:, 0:st] = p_hi
-    p_hl[:, st : 2 * st] = p_hi
-    p_hl[:, 2 * st : 3 * st] = p_lo
+    p_hi, p_lo = halves(jnp.transpose(gain * jnp.exp(-lam * (steps + 1.0))))
+    p_hl[0:st] = p_hi
+    p_hl[st : 2 * st] = p_hi
+    p_hl[2 * st : 3 * st] = p_lo
 
     for h in (1, 0):
         merge_short("kv", h)
@@ -373,11 +373,11 @@
     entry = jnp.where(mine, states_of(leading), 0.0)
     total = jnp.sum(carry + decay_k[nk - 1] * entry, axis=0, keepdims=True)
     st0[...] = total
-    for b in reversed(range(bits)):
+    for b in (3, 4, 2, 1, 0):
 
         @to_later(b)
         def _():
-            for k in groups[b]:
+            for k in sorted(groups[b], key=lambda k: -(k >> 3)):
                 remote(("st", k), st0, st1.at[k], st_ss.at[b], st_rs.at[b], (p ^ k, z))
 
     dscr[0:cs] = leading.astype(f32)
@@ -391,6 +391,11 @@
         line = dscr[pl.ds(c, nk, stride=cs), :].astype(bf16)
         yscr[pl.ds(c, nk, stride=cs), :] = mm(jnp.concatenate([line, line], axis=1), tcat[c])
 
+    def carried(x):
+        x_hi, x_lo = halves(x)
+        return mm(jnp.concatenate([x_hi, x_lo, x_hi], axis=1), p_hl[...])
+
+    yscr[...] += carried(xscr[...])
     tail_in(1, 2 * cs, cs)
     query = short(2 * cs, 0, length)
     into[...] = jnp.zeros_like(into)
@@ -403,11 +408,7 @@
             into[...] += jnp.sum(weight[group] * st1[group], axis=0)
 
     wide = jnp.where(mine, into[...], 0.0)
-    x = jnp.concatenate(
-        [xscr[cs * k : cs * (k + 1)] + decay_k[k] * wide for k in range(nk)], axis=0
-    )
-    x_hi, x_lo = halves(x)
-    y = yscr[...] + mm(jnp.concatenate([x_hi, x_lo, x_hi], axis=1), p_hl[...], NT)
+    y = yscr[...] + carried(jnp.concatenate([decay_k[k] * wide for k in range(nk)], axis=0))
     for k in range(nk):
         sl = slice(cs * k, cs * (k + 1))
         tok = slice(CL * k, CL * (k + 1))
@@ -523,7 +524,7 @@
                 pltpu.VMEM((1, st), f32),
                 pltpu.VMEM((9, cs, CL), f32),
                 pltpu.VMEM((2 * CL, st), bf16),
-                pltpu.VMEM((CL, 3 * st), bf16),
+                pltpu.VMEM((3 * st, CL), bf16),
                 pltpu.VMEM((cs, 2 * CL, CL), bf16),
                 pltpu.VMEM((nk * cs, CL), f32),
                 pltpu.VMEM((nk * cs, CL), f32),

time: 33.9 us -> 33.9 us (level)
  no operation moved by 1% of the time
where the time goes in v10:
time: 33.9 us
  Pallas kernels  33.8 us (100%)
    pallas_call x1, Pallas kernels, body(): pl.pallas_call(functools.partial(conv_kernel, n_seq, n_ch), out_shape=jax...  32.2 us
    pallas_call x1, Pallas kernels, body(): pl.pallas_call(project_kernel, out_shape=jax.ShapeDtypeStruct((w_out.shap...  1.59 us

profile of v10, /device:TPU:24, one launch (start us, length us, event | category | flops | bytes accessed | tf_op | source)
XLA Modules:
  0.0 33.9 jit_solution(4781493883643183317)
XLA Ops:
  0.0 0.0 copy-start
  0.0 32.2 %shard_map.73 = bf16[8,16,1024]{2,1,0:T(8,128)(2,1)S(1)} custom-call(bf16[1024,1024]{1,0:T(8,128)(2,1)} %hid.1, bf16[1024,384]{1,0:T(8,128)(2,1)} %w_in.1, f32[3,48]{1,0:T(4,128)} %taps_in.1, f32[16,16]{1,0:T(8,128)} %rates_in.1, f32[16,16]{1,0:T(8,128)} %res_in.1, f32[1,16]{1,0:T(1,128)} %bitcast.3), custom_call_target="tpu_custom_call" | custom-call | tf_op jit(solution)/shard_map/pallas_call | solution.py:500
  32.3 0.0 copy-done
  32.3 1.6 %shard_map.74 = bf16[1024,1024]{1,0:T(8,128)(2,1)} custom-call(bf16[1024,128]{1,0:T(8,128)(2,1)S(1)} %copy-done, bf16[128,1024]{1,0:T(8,128)(2,1)S(1)} %bitcast.2), custom_call_target="tpu_custom_call" | custom-call | tf_op jit(solution)/shard_map/pallas_call | solution.py:553
Async XLA Ops:
  0.0 32.3 %copy-start = (bf16[1024,128]{1,0:T(8,128)(2,1)S(1)}, bf16[1024,128]{1,0:T(8,128)(2,1)}, u32[]{:S(2)}) copy-start(bf16[1024,128]{1,0:T(8,128)(2,1)} %w_ref.1) | copy-start | bytes 786436
